TPU v7x, 32 devices: a whole 2x2x4 slice. The times are simulated.
32 devices in a mesh: rows: 16 (over z, y, core), cols: 2 (over x).
Axes of the slice: x: 2, y: 2, z: 4, core: 2. Of those that a mesh axis runs over, the one named last changes fastest.
Arguments:
- patches: bfloat16 [128, 128, 512], P('rows', 'cols'), may hold values from -6 to 6
- tissue: int32 [128, 128], P('rows', 'cols'), may hold values 0 or 1
- w_value: bfloat16 [512, 512], replicated, may hold values from -0.25 to 0.25
- w_across: bfloat16 [512, 40], replicated, may hold values from -0.25 to 0.25
- w_down: bfloat16 [512, 40], replicated, may hold values from -0.25 to 0.25
- w_gate: bfloat16 [512, 512], replicated, may hold values from -0.25 to 0.25
- w_out: bfloat16 [512, 512], replicated, may hold values from -0.25 to 0.25
- step_bias_across: float32 [8], replicated, may hold values from -4.5 to -2.5
- step_bias_down: float32 [8], replicated, may hold values from -4.5 to -2.5
- rates_across: float32 [8], replicated, may hold values from 0.015625 to 1
- rates_down: float32 [8], replicated, may hold values from 0.015625 to 1
- skip_across: float32 [8], replicated, may hold values from 0.5 to 1.5
- skip_down: float32 [8], replicated, may hold values from 0.5 to 1.5
- gain_across: float32 [512], replicated, may hold values from 0.5 to 1.5
- gain_final: float32 [512], replicated, may hold values from 0.5 to 1.5
Outputs:
- mixed: bfloat16 [128, 128, 512], P('rows', 'cols')
Inputs may be any that keep to these rules, and one draw needn't show every extreme that they name: 1 marks a tissue patch, 0 background.
All inputs are finite; a program needn't handle non-finite values. No bound on the sum of `tissue` on one device may be relied on, other than what follows from the above.
Results may differ from a plain program's by a relative error of at most 0.015.
Values may be sent and summed in bfloat16 or wider, within the bound.
A program may use at most 64 MiB of HBM per device.

v0:
```python
import math

import jax
import jax.numpy as jnp
from jax import lax
from jax.sharding import PartitionSpec as P

highest = lax.Precision.HIGHEST


def shifted(value, axis, by):
    count = lax.axis_size(axis)
    pairs = [(i, i + by) for i in range(count) if 0 <= i + by < count]
    return lax.ppermute(value, axis, pairs)


def scan_parts(values, b_rows, c_rows, step_sizes, rates, skips):
    line_count, length, head_count, head_width = values.shape
    state_count = b_rows.shape[-1]
    block_len = math.gcd(length, 128)
    block_count = length // block_len
    narrow = values.reshape(line_count, block_count, block_len, head_count, head_width)
    b_blocks = b_rows.reshape(line_count, block_count, block_len, state_count)
    c_blocks = c_rows.reshape(line_count, block_count, block_len, state_count)
    step_blocks = step_sizes.reshape(line_count, block_count, block_len, head_count)
    running = jnp.cumsum(-step_blocks * rates, axis=2)
    causal = (jnp.arange(block_len)[:, None] >= jnp.arange(block_len)[None, :])[
        None, None, :, :, None
    ]
    spans = jnp.where(causal, running[:, :, :, None, :] - running[:, :, None, :, :], 0.0)
    decays = jnp.where(causal, jnp.exp(spans), 0.0)
    intersections = jnp.einsum("lctn,lcsn->lcts", c_blocks, b_blocks, precision=highest)
    weights = (decays * intersections[..., None] * step_blocks[:, :, None, :, :]).astype(
        jnp.bfloat16
    )
    within = jnp.einsum("lctsh,lcshp->lcthp", weights, narrow, preferred_element_type=jnp.float32)
    to_end = jnp.exp(running[:, :, -1:, :] - running) * step_blocks
    push_coef = (b_blocks[..., :, None] * to_end[..., None, :]).astype(jnp.bfloat16)
    pushed = jnp.einsum("lcsnh,lcshp->lchnp", push_coef, narrow, preferred_element_type=jnp.float32)
    totals = running[:, :, -1, :]

    def advance(entered, item):
        pushed_one, total_one = item
        return (jnp.exp(total_one)[..., None, None] * entered + pushed_one, entered)

    final, entering = lax.scan(
        advance,
        jnp.zeros_like(pushed[:, 0]),
        (jnp.moveaxis(pushed, 1, 0), jnp.moveaxis(totals, 1, 0)),
    )
    entering = jnp.moveaxis(entering, 0, 1)
    carried = (
        jnp.einsum("lctn,lchnp->lcthp", c_blocks, entering, precision=highest)
        * jnp.exp(running)[..., None]
    )
    outputs = within + carried + skips[:, None] * narrow.astype(jnp.float32)
    before = jnp.cumsum(totals, axis=1) - totals
    reach = jnp.exp(before[:, :, None, :] + running)
    return (
        outputs.reshape(line_count, length, head_count * head_width),
        final,
        jnp.sum(totals, axis=1),
        reach.reshape(line_count, length, head_count),
    )


def line_scan(values, projected, step_bias, rates, skips):
    head_count = rates.shape[0]
    state_count = (projected.shape[-1] - head_count) // 2
    line_count, length, width_all = values.shape
    b_rows = projected[..., :state_count]
    c_rows = projected[..., state_count : 2 * state_count]
    step_sizes = jax.nn.softplus(projected[..., 2 * state_count :] + step_bias)
    parts = scan_parts(
        values.reshape(line_count, length, head_count, width_all // head_count),
        b_rows,
        c_rows,
        step_sizes,
        rates,
        skips,
    )
    return parts + (c_rows,)


def add_start(outputs, c_rows, reach, start):
    line_count, length, width_all = outputs.shape
    extra = jnp.einsum("ltn,lhnp->lthp", c_rows, start, precision=highest) * reach[..., None]
    return outputs + extra.reshape(line_count, length, width_all)


def rms_norm(values, gain):
    return values * lax.rsqrt(jnp.mean(values * values, axis=-1, keepdims=True) + 1e-05) * gain


def on_device(
    patches,
    tissue,
    w_value,
    w_across,
    w_down,
    w_gate,
    w_out,
    step_bias_across,
    step_bias_down,
    rates_across,
    rates_down,
    skip_across,
    skip_down,
    gain_across,
    gain_final,
):
    masked = patches * tissue.astype(jnp.bfloat16)[..., None]
    values_across = jnp.dot(masked, w_value, preferred_element_type=jnp.float32).astype(
        jnp.bfloat16
    )
    proj_across = jnp.dot(masked, w_across, preferred_element_type=jnp.float32)
    y_across, final, total, reach, c_rows = line_scan(
        values_across, proj_across, step_bias_across, rates_across, skip_across
    )
    decay_all = jnp.exp(total)[..., None, None]

    def relay(turn_index, entered):
        return shifted((decay_all * entered + final).astype(jnp.bfloat16), "cols", 1).astype(
            jnp.float32
        )

    start = lax.fori_loop(0, lax.axis_size("cols") - 1, relay, jnp.zeros_like(final))
    line_out = rms_norm(add_start(y_across, c_rows, reach, start), gain_across).astype(jnp.bfloat16)
    band_shape = line_out.shape
    split_count = lax.axis_size("rows")
    banded = line_out.reshape(
        band_shape[0], split_count, band_shape[1] // split_count, band_shape[2]
    )
    columns = jnp.moveaxis(
        lax.all_to_all(banded, "rows", split_axis=1, concat_axis=0, tiled=True)[:, 0], 1, 0
    )
    proj_down = jnp.dot(columns, w_down, preferred_element_type=jnp.float32)
    y_down = line_scan(columns, proj_down, step_bias_down, rates_down, skip_down)[0]
    column_vals = jnp.moveaxis(y_down.astype(jnp.bfloat16), 0, 1)[:, None]
    column_out = lax.all_to_all(
        column_vals, "rows", split_axis=0, concat_axis=1, tiled=True
    ).reshape(band_shape)
    gate = jnp.dot(masked, w_gate, preferred_element_type=jnp.float32)
    act = (rms_norm(column_out.astype(jnp.float32), gain_final) * jax.nn.silu(gate)).astype(
        jnp.bfloat16
    )
    return (
        masked.astype(jnp.float32) + jnp.dot(act, w_out, preferred_element_type=jnp.float32)
    ).astype(jnp.bfloat16)


def solution(mesh):
    return jax.shard_map(
        on_device,
        mesh=mesh,
        in_specs=(
            P("rows", "cols", None),
            P("rows", "cols"),
            P(),
            P(),
            P(),
            P(),
            P(),
            P(),
            P(),
            P(),
            P(),
            P(),
            P(),
            P(),
            P(),
        ),
        out_specs=P("rows", "cols", None),
        check_vma=False,
    )
```

profile of v0, /device:TPU:0, one launch (start us, length us, event | category | flops | bytes accessed | tf_op | source)
XLA Modules:
  0.0 92.2 jit_solution(2488109731537731661)
XLA Ops:
  0.0 0.8 convert_element_type.95
  0.8 1.5 %fusion.34 = f32[8,64,40]{1,2,0:T(8,128)S(1)} fusion(bf16[8,64,512]{2,1,0:T(8,128)(2,1)} %param.15, bf16[8,64]{1,0:T(8,128)(2,1)S(1)} %convert_element_type.95, bf16[512,40]{0,1:T(8,128)(2,1)} %param.18), kind=kOutput, calls=%fused_computation.49 | convolution fusion | flops 21233664 | bytes 648192 | tf_op jit(solution)/shard_map/dot_general | solution.py:116
  2.2 0.8 multiply_bitcast_fusion
  3.2 6.3 %fusion.69 = f32[8,1,64,8]{3,0,1,2:T(8,128)S(1)} fusion(f32[8,1,64,8]{3,0,1,2:T(8,128)S(1)} %copy.49), kind=kOutput, calls=%fused_computation.98 | output fusion | flops 258048 | bytes 32768 | tf_op jit(solution)/shard_map/jit(cumsum)/reduce_window_sum | solution.py:26
  9.7 0.5 convolution_convert_fusion
  10.2 0.5 reshape.292
  10.8 0.4 fusion.9
  11.2 4.9 %collective-permute-start = (bf16[8,8,16,64]{3,2,1,0:T(8,128)(2,1)S(1)}, bf16[8,8,16,64]{3,2,1,0:T(8,128)(2,1)S(1)}, u32[]{:S(2)}, u32[]{:S(2)}) collective-permute-start(bf16[8,8,16,64]{3,2,1,0:T(8,128)(2,1)S(1)} %fusion.9), channel_id=1, source_target_pairs={{0,1},{2,3},{4,5},{6,7},{8,9},{10,11},{12,13},{14,15},{16,17},{18,... | collective-permute-start | bytes 393224 | tf_op jit(solution)/shard_map/while/body/eval_jaxpr/ppermute | solution.py:14
  16.1 3.1 %fusion.41 = f32[8,64,8,64]{1,3,2,0:T(8,128)} fusion(f32[8,64,40]{1,2,0:T(8,128)S(1)} %fusion.34), kind=kOutput, calls=%fused_computation.55 | convolution fusion | flops 50331648 | bytes 1114112 | tf_op jit(solution)/shard_map/lctn,lchnp->lcthp/dot_general | solution.py:53
  19.2 0.6 fusion.52
  19.8 1.6 %copy.71 = f32[8,64,512]{1,2,0:T(8,128)} copy(bf16[8,64,512]{2,1,0:T(8,128)(2,1)S(1)} %convolution_convert_fusion) | data formatting | bytes 1572864 | tf_op jit(solution)/shard_map/convert_element_type | solution.py:56
  21.6 1.1 %convolution_multiply_fusion = f32[8,64,8,64]{1,3,2,0:T(8,128)S(1)} fusion(bf16[8,8,16,64]{3,2,1,0:T(8,128)(2,1)S(1)} %collective-permute-done, f32[8,64,8]{1,2,0:T(8,128)S(1)} %get-tuple-element.48, f32[8,64,40]{1,2,0:T(8,128)S(1)} %fusion.34), kind=kOutput, calls=%fused_computation.7 | convolution fusion | flops 50593792 | bytes 1409024 | tf_op jit(solution)/shard_map/ltn,lhnp->lthp/dot_general | solution.py:87
  22.7 2.7 %copy.55 = f32[8,64,8,64]{3,2,0,1:T(8,128)} copy(f32[8,64,8,64]{1,3,2,0:T(8,128)S(1)} %convolution_multiply_fusion) | data formatting | bytes 2097152 | tf_op jit(solution)/shard_map/mul | solution.py:87
  25.4 5.4 %fusion.2 = (f32[8,64]{1,0:T(8,128)S(1)}, f32[8,1,64,8,64]{2,4,3,0,1:T(8,128)}) fusion(f32[8,64,8,64]{1,3,2,0:T(8,128)S(1)} %convolution_multiply_fusion, f32[8,1,64,8,64]{2,4,3,0,1:T(8,128)} %bitcast.113, f32[8]{0:T(128)S(1)} %copy-done.4, f32[8,64,8,64]{1,3,2,0:T(8,128)} %fusion.41, f32[8,64,8]{1,2,0:T(8,128)S(1)} %get-tuple-element.49, ...), kind=kOutput, calls=%fused_computation.4 | convolution fusion | flops 36961792 | bytes 4904992 | tf_op jit(solution)/shard_map/lctsh,lcshp->lcthp/dot_general | solution.py:36
  30.8 3.8 %copy.53 = f32[8,1,64,8,64]{4,3,0,2,1:T(8,128)} copy(f32[8,1,64,8,64]{2,4,3,0,1:T(8,128)} %get-tuple-element.58) | data formatting | bytes 2097152 | tf_op jit(solution)/shard_map/add | solution.py:56
  34.6 2.8 %reshape.293 = f32[8,16,4,512]{3,0,2,1:T(8,128)} reshape(f32[8,1,64,8,64]{4,3,0,2,1:T(8,128)} %copy.53) | data formatting | bytes 2097152 | tf_op jit(solution)/shard_map/reshape | solution.py:60
  37.4 1.5 %reshape.294 = f32[8,16,4,512]{3,0,2,1:T(8,128)} reshape(f32[8,64,8,64]{3,2,0,1:T(8,128)S(1)} %copy-done.1) | data formatting | bytes 2097152 | tf_op jit(solution)/shard_map/reshape | solution.py:88
  39.0 2.5 %multiply_convert_fusion.5 = bf16[8,16,4,512]{3,0,2,1:T(8,128)(2,1)} fusion(f32[8,16,4,512]{3,0,2,1:T(8,128)} %reshape.293, f32[8,16,4,512]{3,0,2,1:T(8,128)} %reshape.294, f32[512]{0:T(512)S(1)} %copy-done.3, f32[8,16,4]{0,2,1:T(4,128)S(1)} %bitcast.119), kind=kLoop, calls=%fused_computation.31 | loop fusion | flops 1048576 | bytes 2625536 | tf_op jit(solution)/shard_map/convert_element_type | solution.py:128
  41.5 5.9 %all-to-all-start = ((bf16[8,16,4,512]{3,0,2,1:T(8,128)(2,1)}), bf16[8,16,4,512]{3,0,2,1:T(8,128)(2,1)S(1)}, u32[]{:S(2)}, u32[]{:S(2)}) async-start(bf16[8,16,4,512]{3,0,2,1:T(8,128)(2,1)} %multiply_convert_fusion.5), calls=%async_computation | async-start | bytes 1048576 | tf_op jit(solution)/shard_map/all_to_all | solution.py:135
  47.5 14.4 %all-to-all-done = bf16[8,16,4,512]{3,0,2,1:T(8,128)(2,1)S(1)} async-done(((bf16[8,16,4,512]{3,0,2,1:T(8,128)(2,1)}), bf16[8,16,4,512]{3,0,2,1:T(8,128)(2,1)S(1)}, u32[]{:S(2)}, u32[]{:S(2)}) %all-to-all-start) | async-done | bytes 524320 | tf_op jit(solution)/shard_map/all_to_all | solution.py:135
  61.9 0.3 fusion.54
  62.2 0.6 fusion.57
  63.1 0.3 reduce_window_sum.29
  63.6 1.9 %fusion.3 = f32[4,1,128,8,64]{2,4,3,0,1:T(8,128)} fusion(f32[4,128,8]{1,2,0:T(8,128)S(1)} %copy.62, f32[4,128,40]{1,2,0:T(8,128)S(1)} %fusion.54), kind=kOutput, calls=%fused_computation.10 | convolution fusion | flops 50593792 | bytes 1097728 | tf_op jit(solution)/shard_map/lctn,lchnp->lcthp/dot_general | solution.py:53
  65.7 0.3 copy.58
  65.9 0.3 copy.63
  66.3 2.2 %fusion.6 = bf16[4,1,128,8,64]{2,4,3,0,1:T(8,128)(2,1)S(1)} fusion(f32[4,1,128,8,64]{2,4,3,0,1:T(8,128)} %fusion.3, bf16[4,128,8,64]{1,3,2,0:T(8,128)(2,1)S(1)} %bitcast.117, f32[4,1,128,8,64]{2,4,3,0,1:T(8,128)S(1)} %bitcast.115, f32[4,128,8]{1,2,0:T(8,128)S(1)} %get-tuple-element.36, f32[4,128,128]{2,1,0:T(8,128)S(1)} %fusion.57, ...), kind=kOutput, calls=%fused_computation.17 | convolution fusion | flops 71303168 | bytes 3457056 | tf_op jit(solution)/shard_map/lctsh,lcshp->lcthp/dot_general | solution.py:36
  68.5 0.4 copy.64
  68.9 18.4 %all_to_all.24 = bf16[128,1,4,512]{3,2,1,0:T(4,128)(2,1)S(1)} all-to-all(bf16[128,1,4,512]{3,2,1,0:T(4,128)(2,1)S(1)} %bitcast.114), channel_id=1, replica_groups=mesh['rows'=16,'cols'=2] {'rows'}, dimensions={0} | all-to-all | bytes 1048576 | tf_op jit(solution)/shard_map/all_to_all | solution.py:140
  87.4 0.7 copy.66
  88.1 0.4 reshape.299
  88.9 3.3 %fusion.7 = bf16[8,64,512]{2,1,0:T(8,128)(2,1)} fusion(f32[8,64,512]{2,1,0:T(8,128)S(1)} %reshape.299, bf16[512,512]{1,0:T(8,128)(2,1)} %param.21, bf16[512,512]{1,0:T(8,128)(2,1)} %param.20, f32[512]{0:T(512)S(1)} %copy-done.9, f32[8,64]{1,0:T(8,128)S(1)} %copy.68, bf16[8,64,512]{2,1,0:T(8,128)(2,1)} %param.15, bf16[8,64]{1,0:T(8,128)(2,1)S(1)} %convert_element_type.95), kind=kOutput, calls=%fused_computation.18 | convolution fusion | flops 540803072 | bytes 3150848 | tf_op jit(solution)/shard_map/dot_general | solution.py:148
  (45 shorter events, 1.9 us)
Async XLA Ops:
  0.0 9.7 %copy-start = (bf16[512,512]{1,0:T(8,128)(2,1)S(1)}, bf16[512,512]{1,0:T(8,128)(2,1)}, u32[]{:S(2)}) copy-start(bf16[512,512]{1,0:T(8,128)(2,1)} %param.17) | copy-start | bytes 1572868
  0.0 9.7 %copy-start.7 = (bf16[8,64,512]{2,1,0:T(8,128)(2,1)S(1)}, bf16[8,64,512]{2,1,0:T(8,128)(2,1)}, u32[]{:S(2)}) copy-start(bf16[8,64,512]{2,1,0:T(8,128)(2,1)} %param.15) | copy-start | bytes 1572868
  10.7 9.1 %copy-start.2 = (bf16[8,64,8,64]{3,2,1,0:T(8,128)(2,1)}, bf16[8,64,8,64]{3,2,1,0:T(8,128)(2,1)S(1)}, u32[]{:S(2)}) copy-start(bf16[8,64,8,64]{3,2,1,0:T(8,128)(2,1)S(1)} %reshape.292) | copy-start | bytes 1572868
  11.2 10.4 %collective-permute-start = (bf16[8,8,16,64]{3,2,1,0:T(8,128)(2,1)S(1)}, bf16[8,8,16,64]{3,2,1,0:T(8,128)(2,1)S(1)}, u32[]{:S(2)}, u32[]{:S(2)}) collective-permute-start(bf16[8,8,16,64]{3,2,1,0:T(8,128)(2,1)S(1)} %fusion.9), channel_id=1, source_target_pairs={{0,1},{2,3},{4,5},{6,7},{8,9},{10,11},{12,13},{14,15},{16,17},{18,... | collective-permute-start | bytes 393224 | tf_op jit(solution)/shard_map/while/body/eval_jaxpr/ppermute | solution.py:14
  22.7 2.7 %copy-start.4 = (f32[8]{0:T(128)S(1)}, f32[8]{0:T(128)}, u32[]{:S(2)}) copy-start(f32[8]{0:T(128)} %param.26) | copy-start | bytes 100
  34.6 2.8 %copy-start.1 = (f32[8,64,8,64]{3,2,0,1:T(8,128)S(1)}, f32[8,64,8,64]{3,2,0,1:T(8,128)}, u32[]{:S(2)}) copy-start(f32[8,64,8,64]{3,2,0,1:T(8,128)} %copy.55) | copy-start | bytes 3145732
  37.4 1.6 %copy-start.3 = (f32[512]{0:T(512)S(1)}, f32[512]{0:T(512)}, u32[]{:S(2)}) copy-start(f32[512]{0:T(512)} %param.28) | copy-start | bytes 6148
  38.9 23.1 %copy-start.8 = (bf16[512,40]{0,1:T(8,128)(2,1)S(1)}, bf16[512,40]{0,1:T(8,128)(2,1)}, u32[]{:S(2)}) copy-start(bf16[512,40]{0,1:T(8,128)(2,1)} %param.19) | copy-start | bytes 122884
  39.0 23.8 %copy-start.5 = (f32[8]{0:T(128)S(1)}, f32[8]{0:T(128)}, u32[]{:S(2)}) copy-start(f32[8]{0:T(128)} %param.25) | copy-start | bytes 100
  39.0 23.8 %copy-start.6 = (f32[8]{0:T(128)S(1)}, f32[8]{0:T(128)}, u32[]{:S(2)}) copy-start(f32[8]{0:T(128)} %param.23) | copy-start | bytes 100
  41.5 20.4 %all-to-all-start = ((bf16[8,16,4,512]{3,0,2,1:T(8,128)(2,1)}), bf16[8,16,4,512]{3,0,2,1:T(8,128)(2,1)S(1)}, u32[]{:S(2)}, u32[]{:S(2)}) async-start(bf16[8,16,4,512]{3,0,2,1:T(8,128)(2,1)} %multiply_convert_fusion.5), calls=%async_computation | async-start | bytes 1048576 | tf_op jit(solution)/shard_map/all_to_all | solution.py:135
  65.7 0.7 copy-start.10
  87.4 1.5 %copy-start.9 = (f32[512]{0:T(512)S(1)}, f32[512]{0:T(512)}, u32[]{:S(2)}) copy-start(f32[512]{0:T(512)} %param.29) | copy-start | bytes 6148
where the time goes:
time: 92.6 us; the launch traced here: 92.2 us
  matrix products  20.7 us (22%)
  blocking collectives  18.4 us (20%)
  local copies, waits for them, and re-layouts  16 us (17%)
  waiting for transfers between devices  14.6 us (16%)
  other arithmetic  11.4 us (12%)
  starting transfers between devices  10.8 us (12%)
    all_to_all x1, blocking collectives, on_device(): lax.all_to_all(column_vals, 'rows', split_axis=0, concat_axis=1, tiled=True)  18.4 us
    all_to_all x1, waiting for transfers between devices, on_device(): lax.all_to_all(banded, 'rows', split_axis=1, concat_axis=0, tiled=True)  14.4 us
    dot_general x2, matrix products, scan_parts(): jnp.einsum('lctsh,lcshp->lcthp', weights, narrow, preferred_element_type=...  7.55 us
    another operation x2, other arithmetic, scan_parts(): running = jnp.cumsum(-step_blocks * rates, axis=2)  6.59 us
    all_to_all x1, starting transfers between devices, on_device(): lax.all_to_all(banded, 'rows', split_axis=1, concat_axis=0, tiled=True)  5.94 us
    dot_general x2, matrix products, scan_parts(): jnp.einsum('lctn,lchnp->lcthp', c_blocks, entering, precision=highest)  5.01 us
    ppermute x1, starting transfers between devices, shifted(): return lax.ppermute(value, axis, pairs)  4.86 us
    add x1, local copies, waits for them, and re-layouts, scan_parts(): outputs = within + carried + skips[:, None] * narrow.astype(jnp.float32)  3.79 us
  transfers between devices with their start and end apart: 2, of which 2 were waited for; matrix products, arithmetic and copies ran while one was open for 6% of the time, Pallas kernels for 0%

commit v1 on v0

v1 whole, which is shorter than its diff:
```python
import functools

import jax
import jax.numpy as jnp
from jax import lax
from jax.experimental import pallas as pl
from jax.experimental.pallas import tpu as pltpu
from jax.sharding import PartitionSpec as P

MESH = pl.DeviceIdType.MESH
f32 = jnp.float32
bf16 = jnp.bfloat16


def mm(a, b):
    return jnp.dot(a, b, preferred_element_type=f32)


def mm_nt(a, b):
    return lax.dot_general(a, b, (((1,), (1,)), ((), ())), preferred_element_type=f32)


def mm_tn(a, b):
    return lax.dot_general(a, b, (((0,), (0,)), ((), ())), preferred_element_type=f32)


def parts_of(x):
    high = x.astype(bf16)
    return high, (x - high.astype(f32)).astype(bf16)


def mm_split_right(a, x):
    high, low = parts_of(x)
    return mm(a, high) + mm(a, low)


def mm_split_left(x, b):
    high, low = parts_of(x)
    return mm(high, b) + mm(low, b)


def iota(shape, dim):
    return lax.broadcasted_iota(jnp.int32, shape, dim)


def log2_of(size):
    assert size & (size - 1) == 0
    return size.bit_length() - 1


def one_hot(count, index):
    return jnp.where(iota((count, count), 1) == index, 1.0, 0.0).astype(bf16)


def block_kernel(
    n_rows,
    n_cols,
    patches_ref,
    tissue_ref,
    w_value_ref,
    w_across_ref,
    w_down_ref,
    w_gate_ref,
    w_out_ref,
    bias_a_ref,
    bias_d_ref,
    rates_a_ref,
    rates_d_ref,
    skip_a_ref,
    skip_d_ref,
    gain_a_ref,
    gain_f_ref,
    out_ref,
    masked,
    vals,
    b_all,
    c_all,
    s_exp,
    l_exp,
    y_all,
    gated,
    pushed_all,
    l_end,
    state_out,
    state_in,
    send1,
    recv1,
    send2,
    recv2,
    send_sems,
    recv_sems,
    relay_sems,
):
    local_rows, width, feats = patches_ref.shape
    heads = rates_a_ref.shape[1]
    head_width = feats // heads
    states = (w_across_ref.shape[1] - heads) // 2
    tokens = local_rows * width
    chunk = width
    chunks = tokens // chunk
    per_peer = width // n_rows
    height = n_rows * local_rows
    assert head_width == chunk and height % chunk == 0

    my_row = lax.axis_index("rows")
    my_col = lax.axis_index("cols")

    barrier = pltpu.get_barrier_semaphore()

    @pl.loop(1, n_rows)
    def _(off):
        pl.semaphore_signal(
            barrier,
            inc=1,
            device_id=(lax.rem(my_row + off, n_rows), my_col),
            device_id_type=MESH,
        )

    @pl.when(my_col > 0)
    def _():
        pl.semaphore_signal(
            barrier, inc=1, device_id=(my_row, my_col - 1), device_id_type=MESH
        )

    lane = iota((heads, feats), 1)
    first = iota((heads, feats), 0) * head_width
    expand = jnp.where((lane >= first) & (lane < first + head_width), 1.0, 0.0).astype(bf16)
    place_t = iota((chunk, feats), 0)
    place_u = iota((chunk, feats), 1) & (head_width - 1)
    causal = place_t >= place_u
    diagonal = place_t == place_u
    tri = jnp.where(iota((chunk, chunk), 0) >= iota((chunk, chunk), 1), 1.0, 0.0).astype(bf16)
    group = min(heads, 4)
    gw = group * head_width
    sh = log2_of(head_width)
    same_head = jnp.where(
        lax.shift_right_logical(iota((gw, gw), 0), sh)
        == lax.shift_right_logical(iota((gw, gw), 1), sh),
        1.0,
        0.0,
    ).astype(bf16)

    def wide(ref):
        return mm_split_left(jnp.broadcast_to(ref[...], (8, heads)), expand)[0:1]

    def project(x, w_ref, bias_ref):
        proj = mm(x, w_ref[...])
        b_all[...] = proj[:, :states].astype(bf16)
        c_all[...] = proj[:, states : 2 * states].astype(bf16)
        v = proj[:, 2 * states :] + bias_ref[...]
        steps = jnp.maximum(v, 0.0) + jnp.log1p(jnp.exp(-jnp.abs(v)))
        s_exp[...] = mm_split_left(steps, expand)

    def push(g, neg_rates):
        rows = pl.ds(pl.multiple_of(g * chunk, chunk), chunk)
        s = s_exp[rows, :]
        run = mm_split_right(tri, s * neg_rates)
        end = run[chunk - 1 : chunk, :]
        v = vals[rows, :].astype(f32)
        pushed = mm_tn(b_all[rows, :], (v * (jnp.exp(end - run) * s)).astype(bf16))
        return rows, s, run, end, v, pushed

    def within(rows, s, run, v, skips):
        run_u = jnp.sum(jnp.where(diagonal, run, 0.0), axis=0, keepdims=True)
        s_u = jnp.sum(jnp.where(diagonal, s, 0.0), axis=0, keepdims=True)
        b = b_all[rows, :]
        cb = mm_nt(c_all[rows, :], jnp.concatenate([b] * heads, axis=0))
        decay = jnp.exp(jnp.where(causal, run - run_u, -1e30))
        weights = (decay * cb * s_u).astype(bf16)
        vb = v.astype(bf16)
        outs = []
        for q in range(heads // group):
            lanes = slice(q * gw, (q + 1) * gw)
            stacked = jnp.concatenate([vb[:, lanes]] * group, axis=0) * same_head
            outs.append(mm(weights[:, lanes], stacked))
        return jnp.concatenate(outs, axis=1) + skips * v

    def exchange(slot, source, target):
        def copy_of(off):
            to = lax.rem(my_row + off, n_rows)
            return pltpu.make_async_remote_copy(
                src_ref=source.at[to],
                dst_ref=target.at[my_row],
                send_sem=send_sems.at[slot, off],
                recv_sem=recv_sems.at[slot, off],
                device_id=(to, my_col),
                device_id_type=MESH,
            )

        def start():
            @pl.loop(1, n_rows)
            def _(off):
                copy_of(off).start()

            target[my_row] = source[my_row]

        def finish():
            @pl.loop(1, n_rows)
            def _(off):
                came = lax.rem(my_row + n_rows - off, n_rows)
                pltpu.make_async_remote_copy(
                    src_ref=source.at[came],
                    dst_ref=target.at[came],
                    send_sem=send_sems.at[slot, off],
                    recv_sem=recv_sems.at[slot, off],
                    device_id=(came, my_col),
                    device_id_type=MESH,
                ).wait_recv()

        def drain():
            @pl.loop(1, n_rows)
            def _(off):
                copy_of(off).wait_send()

        return start, finish, drain

    def put(ref, x):
        if ref.shape[1] % 16:
            x = x.astype(f32).reshape(ref.shape).astype(bf16)
        else:
            x = x.astype(bf16).reshape(ref.shape)
        ref[...] = x

    def take(ref):
        x = ref[...]
        if ref.shape[1] % 16:
            return x.astype(f32).reshape(tokens, feats).astype(bf16)
        return x.reshape(tokens, feats)

    flags = tissue_ref[...].astype(f32).T
    for r in range(local_rows):
        flag = jnp.broadcast_to(flags[:, r : r + 1], (width, feats)) > 0.5
        masked[r * width : (r + 1) * width, :] = jnp.where(
            flag, patches_ref[r].astype(f32), 0.0
        ).astype(bf16)

    x = masked[...]
    vals[...] = mm(x, w_value_ref[...]).astype(bf16)
    project(x, w_across_ref, bias_a_ref)
    neg_rates = -wide(rates_a_ref)
    skips = wide(skip_a_ref)

    @pl.loop(0, chunks)
    def _(g):
        rows, _, run, end, _, pushed = push(g, neg_rates)
        l_exp[rows, :] = run
        l_end[g] = end
        pushed_all[g] = pushed

    greeted = n_rows - 1 + jnp.where(my_col < n_cols - 1, 1, 0)
    pl.semaphore_wait(barrier, greeted)

    relay = pltpu.make_async_remote_copy(
        src_ref=state_out,
        dst_ref=state_in,
        send_sem=relay_sems.at[0],
        recv_sem=relay_sems.at[1],
        device_id=(my_row, lax.rem(my_col + 1, n_cols)),
        device_id_type=MESH,
    )

    @pl.when(my_col == 0)
    def _():
        state_in[...] = jnp.zeros_like(state_in)
        if n_cols > 1:
            state_out[...] = pushed_all[...].astype(bf16)
            relay.start()

    @pl.loop(0, chunks)
    def _(g):
        rows = pl.ds(pl.multiple_of(g * chunk, chunk), chunk)
        y_all[rows, :] = within(
            rows, s_exp[rows, :], l_exp[rows, :], vals[rows, :].astype(f32), skips
        )

    @pl.when(my_col > 0)
    def _():
        relay.wait_recv()

        @pl.when(my_col < n_cols - 1)
        def _():
            state_out[...] = (
                pushed_all[...] + jnp.exp(l_end[...]) * state_in[...].astype(f32)
            ).astype(bf16)
            relay.start()

    gain_a = gain_a_ref[...]

    @pl.loop(0, chunks)
    def _(g):
        rows = pl.ds(pl.multiple_of(g * chunk, chunk), chunk)
        y = y_all[rows, :] + mm(c_all[rows, :], state_in[g]) * jnp.exp(l_exp[rows, :])
        scale = lax.rsqrt(jnp.mean(y * y, axis=-1, keepdims=True) + 1e-5)
        vals[rows, :] = (y * scale * gain_a).astype(bf16)

    rsh = log2_of(local_rows)
    csh = log2_of(width)
    m = iota((tokens, tokens), 0)
    by_col = one_hot(
        tokens,
        ((m & (local_rows - 1)) << csh) + lax.shift_right_logical(m, rsh),
    )
    put(send1, mm(by_col, vals[...]))
    start1, finish1, drain1 = exchange(0, send1, recv1)
    start1()

    gate = mm(masked[...], w_gate_ref[...])
    gated[...] = gate / (1.0 + jnp.exp(-gate)) * gain_f_ref[...]
    neg_rates_d = -wide(rates_d_ref)
    skips_d = wide(skip_d_ref)
    hsh = log2_of(height)
    psh = log2_of(per_peer)
    m = iota((tokens, tokens), 0)
    c_of = lax.shift_right_logical(m, hsh)
    i_of = m & (height - 1)
    to_columns = one_hot(
        tokens,
        (lax.shift_right_logical(i_of, rsh) << (rsh + psh))
        + (c_of << rsh)
        + (i_of & (local_rows - 1)),
    )

    @pl.when(my_col < n_cols - 1)
    def _():
        relay.wait_send()

    finish1()
    cols = mm(to_columns, take(recv1)).astype(bf16)
    vals[...] = cols
    project(cols, w_down_ref, bias_d_ref)

    per_line = height // chunk

    def line(c, _):
        def step(k, entered):
            g = c * per_line + k
            rows, s, run, end, v, pushed = push(g, neg_rates_d)
            y = within(rows, s, run, v, skips_d)
            y = y + mm(c_all[rows, :], entered.astype(bf16)) * jnp.exp(run)
            vals[rows, :] = y.astype(bf16)
            return jnp.exp(end) * entered + pushed

        lax.fori_loop(0, per_line, step, jnp.zeros((states, feats), f32))
        return 0

    lax.fori_loop(0, per_peer, line, 0)
    put(send2, mm_tn(to_columns, vals[...]))
    start2, finish2, drain2 = exchange(1, send2, recv2)
    start2()
    drain1()
    finish2()
    z = mm_tn(by_col, take(recv2))
    scale = lax.rsqrt(jnp.mean(z * z, axis=-1, keepdims=True) + 1e-5)
    act = (z * scale * gated[...]).astype(bf16)
    mixed = masked[...].astype(f32) + mm(act, w_out_ref[...])
    out_ref[...] = mixed.astype(bf16).reshape(out_ref.shape)
    drain2()


def on_device(n_rows, n_cols, *args):
    args = [a.reshape(1, -1) if a.ndim == 1 else a for a in args]
    patches = args[0]
    local_rows, width, feats = patches.shape
    tokens = local_rows * width
    heads = args[9].shape[1]
    states = (args[3].shape[1] - heads) // 2
    chunks = local_rows
    piece = (n_rows, local_rows * (width // n_rows), feats)
    big = (tokens, feats)
    vmem = pl.BlockSpec(memory_space=pltpu.VMEM)
    return pl.pallas_call(
        functools.partial(block_kernel, n_rows, n_cols),
        out_shape=jax.ShapeDtypeStruct(patches.shape, bf16),
        in_specs=[vmem] * len(args),
        out_specs=vmem,
        scratch_shapes=[
            pltpu.VMEM(big, bf16),
            pltpu.VMEM(big, bf16),
            pltpu.VMEM((tokens, states), bf16),
            pltpu.VMEM((tokens, states), bf16),
            pltpu.VMEM(big, f32),
            pltpu.VMEM(big, f32),
            pltpu.VMEM(big, f32),
            pltpu.VMEM(big, f32),
            pltpu.VMEM((chunks, states, feats), f32),
            pltpu.VMEM((chunks, 1, feats), f32),
            pltpu.VMEM((chunks, states, feats), bf16),
            pltpu.VMEM((chunks, states, feats), bf16),
            pltpu.VMEM(piece, bf16),
            pltpu.VMEM(piece, bf16),
            pltpu.VMEM(piece, bf16),
            pltpu.VMEM(piece, bf16),
            pltpu.SemaphoreType.DMA((2, n_rows)),
            pltpu.SemaphoreType.DMA((2, n_rows)),
            pltpu.SemaphoreType.DMA((2,)),
        ],
        compiler_params=pltpu.CompilerParams(
            collective_id=0, has_side_effects=True, vmem_limit_bytes=40 * 1024 * 1024
        ),
    )(*args)


def solution(mesh):
    rep = P()
    return jax.shard_map(
        functools.partial(on_device, mesh.shape["rows"], mesh.shape["cols"]),
        mesh=mesh,
        in_specs=(P("rows", "cols", None), P("rows", "cols")) + (rep,) * 13,
        out_specs=P("rows", "cols", None),
        check_vma=False,
    )
```

time: 92.6 us -> 51.2 us (0.55)
  the two profiles are of different devices: /device:TPU:0 before, /device:TPU:31 now
where the time goes in v1:
time: 51.2 us; the launch traced here: 50.8 us
  Pallas kernels  44.1 us (86%)
  local copies, waits for them, and re-layouts  6.57 us (13%)
    pallas_call x1, Pallas kernels, on_device(): pl.pallas_call(functools.partial(block_kernel, n_rows, n_cols), out_shape...  44.1 us
    unnamed x31, local copies, waits for them, and re-layouts  6.57 us

profile of v1, /device:TPU:31, one launch (start us, length us, event | category | flops | bytes accessed | tf_op | source)
XLA Modules:
  0.0 50.8 jit_solution(5294903355792517935)
XLA Ops:
  0.0 0.0 copy-start.13
  0.0 0.9 %copy.16.w_across_ref = bf16[512,40]{1,0:T(8,128)(2,1)S(1)} copy(bf16[512,40]{0,1:T(8,128)(2,1)} %param.18) | data formatting | bytes 81920 | tf_op args[3]
  0.9 0.0 copy-done.13
  0.9 0.0 copy-start.4
  0.9 0.0 copy-start.5
  0.9 0.0 copy-start.6
  1.0 0.0 copy-start.7
  1.0 0.0 copy-start.8
  1.0 0.0 copy-start.9
  1.0 0.0 copy-start.10
  1.0 0.0 copy-start.11
  1.0 0.0 copy-start.12
  1.0 0.1 copy.17.w_down_ref
  1.2 0.5 copy-done.4
  1.6 0.0 copy-done.5
  1.6 0.0 copy-done.6
  1.6 0.0 copy-done.7
  1.6 0.0 copy-done.8
  1.6 0.0 copy-done.9
  1.7 0.0 copy-done.10
  1.7 0.0 copy-done.11
  1.7 0.0 copy-done.12
  1.7 0.0 copy-start
  1.7 1.0 %copy-done = bf16[8,64,512]{2,1,0:T(8,128)(2,1)S(1)} copy-done((bf16[8,64,512]{2,1,0:T(8,128)(2,1)S(1)}, bf16[8,64,512]{2,1,0:T(8,128)(2,1)}, u32[]{:S(2)}) %copy-start) | copy-done | bytes 524312
  2.7 0.0 copy-start.1
  2.8 1.0 %copy-done.1 = bf16[512,512]{1,0:T(8,128)(2,1)S(1)} copy-done((bf16[512,512]{1,0:T(8,128)(2,1)S(1)}, bf16[512,512]{1,0:T(8,128)(2,1)}, u32[]{:S(2)}) %copy-start.1) | copy-done | bytes 524312
  3.8 0.0 copy-start.2
  3.8 1.0 %copy-done.2 = bf16[512,512]{1,0:T(8,128)(2,1)S(1)} copy-done((bf16[512,512]{1,0:T(8,128)(2,1)S(1)}, bf16[512,512]{1,0:T(8,128)(2,1)}, u32[]{:S(2)}) %copy-start.2) | copy-done | bytes 524312
  4.8 0.0 copy-start.3
  4.8 1.0 %copy-done.3 = bf16[512,512]{1,0:T(8,128)(2,1)S(1)} copy-done((bf16[512,512]{1,0:T(8,128)(2,1)S(1)}, bf16[512,512]{1,0:T(8,128)(2,1)}, u32[]{:S(2)}) %copy-start.3) | copy-done | bytes 524312
  5.9 44.1 %shard_map.145 = bf16[8,64,512]{2,1,0:T(8,128)(2,1)S(1)} custom-call(bf16[8,64,512]{2,1,0:T(8,128)(2,1)S(1)} %copy-done, s32[8,64]{1,0:T(8,128)S(1)} %copy-done.4, bf16[512,512]{1,0:T(8,128)(2,1)S(1)} %copy-done.1, bf16[512,40]{1,0:T(8,128)(2,1)S(1)} %copy.16.w_across_ref, bf16[512,40]{1,0:T(8,128)(2,1)S(1)} %copy.17.w_down_ref, ...), custom_call_target="tpu_custom_call" | custom-call | tf_op jit(solution)/shard_map/pallas_call | solution.py:371
  50.0 0.8 %copy.19 = bf16[8,64,512]{2,1,0:T(8,128)(2,1)} copy(bf16[8,64,512]{2,1,0:T(8,128)(2,1)S(1)} %shard_map.145) | data formatting | bytes 1048576
Async XLA Ops:
  0.0 0.9 %copy-start.13 = (bf16[512,40]{0,1:T(8,128)(2,1)S(1)}, bf16[512,40]{0,1:T(8,128)(2,1)}, u32[]{:S(2)}) copy-start(bf16[512,40]{0,1:T(8,128)(2,1)} %param.19) | copy-start | bytes 122884
  0.9 0.7 %copy-start.4 = (s32[8,64]{1,0:T(8,128)S(1)}, s32[8,64]{1,0:T(8,128)}, u32[]{:S(2)}) copy-start(s32[8,64]{1,0:T(8,128)} %tissue_ref.1) | copy-start | bytes 6148
  0.9 0.7 %copy-start.5 = (f32[512]{0:T(512)S(1)}, f32[512]{0:T(512)}, u32[]{:S(2)}) copy-start(f32[512]{0:T(512)} %param.28) | copy-start | bytes 6148
  0.9 0.7 %copy-start.6 = (f32[512]{0:T(512)S(1)}, f32[512]{0:T(512)}, u32[]{:S(2)}) copy-start(f32[512]{0:T(512)} %param.29) | copy-start | bytes 6148
  1.0 0.7 %copy-start.7 = (f32[8]{0:T(128)S(1)}, f32[8]{0:T(128)}, u32[]{:S(2)}) copy-start(f32[8]{0:T(128)} %param.22) | copy-start | bytes 100
  1.0 0.7 %copy-start.8 = (f32[8]{0:T(128)S(1)}, f32[8]{0:T(128)}, u32[]{:S(2)}) copy-start(f32[8]{0:T(128)} %param.23) | copy-start | bytes 100
  1.0 0.7 %copy-start.9 = (f32[8]{0:T(128)S(1)}, f32[8]{0:T(128)}, u32[]{:S(2)}) copy-start(f32[8]{0:T(128)} %param.24) | copy-start | bytes 100
  1.0 0.7 %copy-start.10 = (f32[8]{0:T(128)S(1)}, f32[8]{0:T(128)}, u32[]{:S(2)}) copy-start(f32[8]{0:T(128)} %param.25) | copy-start | bytes 100
  1.0 0.7 %copy-start.11 = (f32[8]{0:T(128)S(1)}, f32[8]{0:T(128)}, u32[]{:S(2)}) copy-start(f32[8]{0:T(128)} %param.26) | copy-start | bytes 100
  1.0 0.7 %copy-start.12 = (f32[8]{0:T(128)S(1)}, f32[8]{0:T(128)}, u32[]{:S(2)}) copy-start(f32[8]{0:T(128)} %param.27) | copy-start | bytes 100
  1.7 1.0 %copy-start = (bf16[8,64,512]{2,1,0:T(8,128)(2,1)S(1)}, bf16[8,64,512]{2,1,0:T(8,128)(2,1)}, u32[]{:S(2)}) copy-start(bf16[8,64,512]{2,1,0:T(8,128)(2,1)} %patches_ref.1) | copy-start | bytes 1572868
  2.7 1.0 %copy-start.1 = (bf16[512,512]{1,0:T(8,128)(2,1)S(1)}, bf16[512,512]{1,0:T(8,128)(2,1)}, u32[]{:S(2)}) copy-start(bf16[512,512]{1,0:T(8,128)(2,1)} %w_value_ref.1) | copy-start | bytes 1572868
  3.8 1.0 %copy-start.2 = (bf16[512,512]{1,0:T(8,128)(2,1)S(1)}, bf16[512,512]{1,0:T(8,128)(2,1)}, u32[]{:S(2)}) copy-start(bf16[512,512]{1,0:T(8,128)(2,1)} %w_gate_ref.1) | copy-start | bytes 1572868
  4.8 1.0 %copy-start.3 = (bf16[512,512]{1,0:T(8,128)(2,1)S(1)}, bf16[512,512]{1,0:T(8,128)(2,1)}, u32[]{:S(2)}) copy-start(bf16[512,512]{1,0:T(8,128)(2,1)} %w_out_ref.1) | copy-start | bytes 1572868

commit v2 on v1

--- a/solution.py
+++ b/solution.py
@@ -48,53 +48,94 @@
     return size.bit_length() - 1
 
 
-def one_hot(count, index):
-    return jnp.where(iota((count, count), 1) == index, 1.0, 0.0).astype(bf16)
+def one_hot(index):
+    count, lanes = index.shape
+    lane = iota(index.shape, 1)
+    tiles = [
+        jnp.where(index - start == lane, 1.0, 0.0).astype(bf16)
+        for start in range(0, count, lanes)
+    ]
+    return jnp.concatenate(tiles, axis=1)
+
+
+ARGS = (
+    "patches",
+    "tissue",
+    "w_value",
+    "w_across",
+    "w_down",
+    "w_gate",
+    "w_out",
+    "bias_a",
+    "bias_d",
+    "rates_a",
+    "rates_d",
+    "skip_a",
+    "skip_d",
+    "gain_a",
+    "gain_f",
+)
+SMALL = ARGS[7:]
+LOAD_ORDER = ("tissue", "patches", "w_value", "w_across") + SMALL + ("w_gate", "w_down", "w_out")
 
 
 def block_kernel(
     n_rows,
     n_cols,
-    patches_ref,
-    tissue_ref,
-    w_value_ref,
-    w_across_ref,
-    w_down_ref,
-    w_gate_ref,
-    w_out_ref,
-    bias_a_ref,
-    bias_d_ref,
-    rates_a_ref,
-    rates_d_ref,
-    skip_a_ref,
-    skip_d_ref,
-    gain_a_ref,
-    gain_f_ref,
-    out_ref,
-    masked,
-    vals,
-    b_all,
-    c_all,
-    s_exp,
-    l_exp,
-    y_all,
-    gated,
-    pushed_all,
-    l_end,
-    state_out,
-    state_in,
-    send1,
-    recv1,
-    send2,
-    recv2,
-    send_sems,
-    recv_sems,
-    relay_sems,
+    *refs,
 ):
+    count = len(ARGS)
+    sources, out_ref, held = refs[:count], refs[count], refs[count + 1 : 2 * count + 1]
+    (
+        masked,
+        vals,
+        b_all,
+        c_all,
+        bt_all,
+        v_all,
+        l_exp,
+        y_all,
+        gated,
+        pushed_all,
+        l_end,
+        state_out,
+        state_in,
+        send1,
+        recv1,
+        send2,
+        recv2,
+        send_sems,
+        recv_sems,
+        relay_sems,
+        load_sems,
+    ) = refs[2 * count + 1 :]
+    loads = {
+        name: pltpu.make_async_copy(sources[k], held[k], load_sems.at[k])
+        for k, name in enumerate(ARGS)
+    }
+    for name in LOAD_ORDER:
+        loads[name].start()
+    (
+        patches_ref,
+        tissue_ref,
+        w_value_ref,
+        w_across_ref,
+        w_down_ref,
+        w_gate_ref,
+        w_out_ref,
+        bias_a_ref,
+        bias_d_ref,
+        rates_a_ref,
+        rates_d_ref,
+        skip_a_ref,
+        skip_d_ref,
+        gain_a_ref,
+        gain_f_ref,
+    ) = held
     local_rows, width, feats = patches_ref.shape
     heads = rates_a_ref.shape[1]
     head_width = feats // heads
-    states = (w_across_ref.shape[1] - heads) // 2
+    states = (w_across_ref.shape[0] - heads) // 2
     tokens = local_rows * width
     chunk = width
     chunks = tokens // chunk
@@ -129,7 +170,17 @@
     place_u = iota((chunk, feats), 1) & (head_width - 1)
     causal = place_t >= place_u
     diagonal = place_t == place_u
-    tri = jnp.where(iota((chunk, chunk), 0) >= iota((chunk, chunk), 1), 1.0, 0.0).astype(bf16)
+    pair = 2 if chunks % 2 == 0 else 1
+    span = pair * chunk
+    tri_t, tri_u = iota((span, span), 0), iota((span, span), 1)
+    csh = log2_of(chunk)
+    tri = jnp.where(
+        (tri_t >= tri_u)
+        & (lax.shift_right_logical(tri_t, csh) == lax.shift_right_logical(tri_u, csh)),
+        1.0,
+        0.0,
+    ).astype(bf16)
+    tri = jnp.concatenate([tri, tri], axis=1)
     group = min(heads, 4)
     gw = group * head_width
     sh = log2_of(head_width)
@@ -143,37 +194,54 @@
     def wide(ref):
         return mm_split_left(jnp.broadcast_to(ref[...], (8, heads)), expand)[0:1]
 
-    def project(x, w_ref, bias_ref):
-        proj = mm(x, w_ref[...])
+    def tall(ref):
+        square = jnp.broadcast_to(ref[...], (heads, heads))
+        eye = iota((heads, heads), 0) == iota((heads, heads), 1)
+        return jnp.sum(jnp.where(eye, square, 0.0), axis=1, keepdims=True)
+
+    def spread(x):
+        high, low = parts_of(x)
+        return mm_tn(
+            jnp.concatenate([high, low], axis=0), jnp.concatenate([expand, expand], axis=0)
+        )
+
+    def project(x, w_ref, bias, neg_rates):
+        weights = w_ref[...]
+        proj = mm_nt(x, weights[: 2 * states])
         b_all[...] = proj[:, :states].astype(bf16)
-        c_all[...] = proj[:, states : 2 * states].astype(bf16)
-        v = proj[:, 2 * states :] + bias_ref[...]
+        c_all[...] = proj[:, states:].astype(bf16)
+        turned = mm_nt(weights, x)
+        bt_all[...] = turned[:states].astype(bf16)
+        v = turned[2 * states :] + bias
         steps = jnp.maximum(v, 0.0) + jnp.log1p(jnp.exp(-jnp.abs(v)))
-        s_exp[...] = mm_split_left(steps, expand)
-
-    def push(g, neg_rates):
-        rows = pl.ds(pl.multiple_of(g * chunk, chunk), chunk)
-        s = s_exp[rows, :]
-        run = mm_split_right(tri, s * neg_rates)
+        v_all[...] = (spread(steps) * vals[...].astype(f32)).astype(bf16)
+        high, low = parts_of(spread(steps * neg_rates))
+        for g in range(0, chunks, pair):
+            rows = slice(g * chunk, (g + pair) * chunk)
+            l_exp[rows, :] = mm(tri, jnp.concatenate([high[rows], low[rows]], axis=0))
+
+    def push(g):
+        rows = slice(g * chunk, (g + 1) * chunk)
+        run = l_exp[rows, :]
         end = run[chunk - 1 : chunk, :]
-        v = vals[rows, :].astype(f32)
-        pushed = mm_tn(b_all[rows, :], (v * (jnp.exp(end - run) * s)).astype(bf16))
-        return rows, s, run, end, v, pushed
-
-    def within(rows, s, run, v, skips):
+        scaled = v_all[rows, :].astype(f32) * jnp.exp(end - run)
+        return end, mm(bt_all[:, rows], scaled.astype(bf16))
+
+    def within(g, skips):
+        rows = slice(g * chunk, (g + 1) * chunk)
+        run = l_exp[rows, :]
         run_u = jnp.sum(jnp.where(diagonal, run, 0.0), axis=0, keepdims=True)
-        s_u = jnp.sum(jnp.where(diagonal, s, 0.0), axis=0, keepdims=True)
         b = b_all[rows, :]
         cb = mm_nt(c_all[rows, :], jnp.concatenate([b] * heads, axis=0))
         decay = jnp.exp(jnp.where(causal, run - run_u, -1e30))
-        weights = (decay * cb * s_u).astype(bf16)
-        vb = v.astype(bf16)
+        weights = (decay * cb).astype(bf16)
+        vb = v_all[rows, :]
         outs = []
         for q in range(heads // group):
             lanes = slice(q * gw, (q + 1) * gw)
             stacked = jnp.concatenate([vb[:, lanes]] * group, axis=0) * same_head
             outs.append(mm(weights[:, lanes], stacked))
-        return jnp.concatenate(outs, axis=1) + skips * v
+        return jnp.concatenate(outs, axis=1) + skips * vals[rows, :].astype(f32)
 
     def exchange(slot, source, target):
         def copy_of(off):
@@ -227,6 +295,20 @@
             return x.astype(f32).reshape(tokens, feats).astype(bf16)
         return x.reshape(tokens, feats)
 
+    rsh = log2_of(local_rows)
+    hsh = log2_of(height)
+    psh = log2_of(per_peer)
+    m = iota((tokens, 128), 0)
+    by_col = one_hot(((m & (local_rows - 1)) << csh) + lax.shift_right_logical(m, rsh))
+    i_of = m & (height - 1)
+    to_columns = one_hot(
+        (lax.shift_right_logical(i_of, rsh) << (rsh + psh))
+        + (lax.shift_right_logical(m, hsh) << rsh)
+        + (i_of & (local_rows - 1))
+    )
+
+    loads["tissue"].wait()
+    loads["patches"].wait()
     flags = tissue_ref[...].astype(f32).T
     for r in range(local_rows):
         flag = jnp.broadcast_to(flags[:, r : r + 1], (width, feats)) > 0.5
@@ -234,18 +316,15 @@
             flag, patches_ref[r].astype(f32), 0.0
         ).astype(bf16)
 
+    for name in ("w_value", "w_across") + SMALL:
+        loads[name].wait()
     x = masked[...]
     vals[...] = mm(x, w_value_ref[...]).astype(bf16)
-    project(x, w_across_ref, bias_a_ref)
-    neg_rates = -wide(rates_a_ref)
+    project(x, w_across_ref, tall(bias_a_ref), -tall(rates_a_ref))
     skips = wide(skip_a_ref)
 
-    @pl.loop(0, chunks)
-    def _(g):
-        rows, _, run, end, _, pushed = push(g, neg_rates)
-        l_exp[rows, :] = run
-        l_end[g] = end
-        pushed_all[g] = pushed
+    for g in range(chunks):
+        l_end[g], pushed_all[g] = push(g)
 
     greeted = n_rows - 1 + jnp.where(my_col < n_cols - 1, 1, 0)
     pl.semaphore_wait(barrier, greeted)
@@ -266,12 +345,8 @@
             state_out[...] = pushed_all[...].astype(bf16)
             relay.start()
 
-    @pl.loop(0, chunks)
-    def _(g):
-        rows = pl.ds(pl.multiple_of(g * chunk, chunk), chunk)
-        y_all[rows, :] = within(
-            rows, s_exp[rows, :], l_exp[rows, :], vals[rows, :].astype(f32), skips
-        )
+    for g in range(chunks):
+        y_all[g * chunk : (g + 1) * chunk, :] = within(g, skips)
 
     @pl.when(my_col > 0)
     def _():
@@ -285,40 +360,23 @@
             relay.start()
 
     gain_a = gain_a_ref[...]
-
-    @pl.loop(0, chunks)
-    def _(g):
-        rows = pl.ds(pl.multiple_of(g * chunk, chunk), chunk)
+    for g in range(chunks):
+        rows = slice(g * chunk, (g + 1) * chunk)
         y = y_all[rows, :] + mm(c_all[rows, :], state_in[g]) * jnp.exp(l_exp[rows, :])
         scale = lax.rsqrt(jnp.mean(y * y, axis=-1, keepdims=True) + 1e-5)
         vals[rows, :] = (y * scale * gain_a).astype(bf16)
 
-    rsh = log2_of(local_rows)
-    csh = log2_of(width)
-    m = iota((tokens, tokens), 0)
-    by_col = one_hot(
-        tokens,
-        ((m & (local_rows - 1)) << csh) + lax.shift_right_logical(m, rsh),
-    )
     put(send1, mm(by_col, vals[...]))
     start1, finish1, drain1 = exchange(0, send1, recv1)
     start1()
 
+    loads["w_gate"].wait()
     gate = mm(masked[...], w_gate_ref[...])
     gated[...] = gate / (1.0 + jnp.exp(-gate)) * gain_f_ref[...]
-    neg_rates_d = -wide(rates_d_ref)
     skips_d = wide(skip_d_ref)
-    hsh = log2_of(height)
-    psh = log2_of(per_peer)
-    m = iota((tokens, tokens), 0)
-    c_of = lax.shift_right_logical(m, hsh)
-    i_of = m & (height - 1)
-    to_columns = one_hot(
-        tokens,
-        (lax.shift_right_logical(i_of, rsh) << (rsh + psh))
-        + (c_of << rsh)
-        + (i_of & (local_rows - 1)),
-    )
+    bias_d, neg_rates_d = tall(bias_d_ref), -tall(rates_d_ref)
+    loads["w_down"].wait()
+    loads["w_out"].wait()
 
     @pl.when(my_col < n_cols - 1)
     def _():
@@ -327,24 +385,23 @@
     finish1()
     cols = mm(to_columns, take(recv1)).astype(bf16)
     vals[...] = cols
-    project(cols, w_down_ref, bias_d_ref)
+    project(cols, w_down_ref, bias_d, neg_rates_d)
 
     per_line = height // chunk
-
-    def line(c, _):
-        def step(k, entered):
-            g = c * per_line + k
-            rows, s, run, end, v, pushed = push(g, neg_rates_d)
-            y = within(rows, s, run, v, skips_d)
-            y = y + mm(c_all[rows, :], entered.astype(bf16)) * jnp.exp(run)
-            vals[rows, :] = y.astype(bf16)
-            return jnp.exp(end) * entered + pushed
-
-        lax.fori_loop(0, per_line, step, jnp.zeros((states, feats), f32))
-        return 0
-
-    lax.fori_loop(0, per_peer, line, 0)
-    put(send2, mm_tn(to_columns, vals[...]))
+    for c in range(per_peer):
+        entered = None
+        for g in range(c * per_line, (c + 1) * per_line):
+            rows = slice(g * chunk, (g + 1) * chunk)
+            end, pushed = push(g)
+            y = within(g, skips_d)
+            if entered is None:
+                entered = pushed
+            else:
+                y = y + mm(c_all[rows, :], entered.astype(bf16)) * jnp.exp(l_exp[rows, :])
+                entered = jnp.exp(end) * entered + pushed
+            y_all[rows, :] = y
+
+    put(send2, mm_tn(to_columns, y_all[...].astype(bf16)))
     start2, finish2, drain2 = exchange(1, send2, recv2)
     start2()
     drain1()
@@ -359,11 +416,12 @@
 
 def on_device(n_rows, n_cols, *args):
     args = [a.reshape(1, -1) if a.ndim == 1 else a for a in args]
+    args[3], args[4] = args[3].T, args[4].T
     patches = args[0]
     local_rows, width, feats = patches.shape
     tokens = local_rows * width
     heads = args[9].shape[1]
-    states = (args[3].shape[1] - heads) // 2
+    states = (args[3].shape[0] - heads) // 2
     chunks = local_rows
     piece = (n_rows, local_rows * (width // n_rows), feats)
     big = (tokens, feats)
@@ -371,14 +429,16 @@
     return pl.pallas_call(
         functools.partial(block_kernel, n_rows, n_cols),
         out_shape=jax.ShapeDtypeStruct(patches.shape, bf16),
-        in_specs=[vmem] * len(args),
+        in_specs=[pl.BlockSpec(memory_space=pl.ANY)] * len(args),
         out_specs=vmem,
-        scratch_shapes=[
+        scratch_shapes=[pltpu.VMEM(a.shape, a.dtype) for a in args]
+        + [
             pltpu.VMEM(big, bf16),
             pltpu.VMEM(big, bf16),
             pltpu.VMEM((tokens, states), bf16),
             pltpu.VMEM((tokens, states), bf16),
-            pltpu.VMEM(big, f32),
+            pltpu.VMEM((states, tokens), bf16),
+            pltpu.VMEM(big, bf16),
             pltpu.VMEM(big, f32),
             pltpu.VMEM(big, f32),
             pltpu.VMEM(big, f32),
@@ -393,9 +453,10 @@
             pltpu.SemaphoreType.DMA((2, n_rows)),
             pltpu.SemaphoreType.DMA((2, n_rows)),
             pltpu.SemaphoreType.DMA((2,)),
+            pltpu.SemaphoreType.DMA((len(args),)),
         ],
         compiler_params=pltpu.CompilerParams(
-            collective_id=0, has_side_effects=True, vmem_limit_bytes=40 * 1024 * 1024
+            collective_id=0, has_side_effects=True, vmem_limit_bytes=56 * 1024 * 1024
         ),
     )(*args)
 

time: 51.2 us -> 40.9 us (0.80)
  the two profiles are of different devices: /device:TPU:31 before, /device:TPU:27 now
where the time goes in v2:
time: 40.9 us; the launch traced here: 40.8 us
  Pallas kernels  38.9 us (95%)
  local copies, waits for them, and re-layouts  1.87 us (5%)
    pallas_call x1, Pallas kernels, on_device(): pl.pallas_call(functools.partial(block_kernel, n_rows, n_cols), out_shape...  38.9 us
    unnamed x1, local copies, waits for them, and re-layouts  1.87 us

profile of v2, /device:TPU:27, one launch (start us, length us, event | category | flops | bytes accessed | tf_op | source)
XLA Modules:
  0.0 40.8 jit_solution(4307470321868245526)
XLA Ops:
  0.0 38.9 %shard_map.145 = bf16[8,64,512]{2,1,0:T(8,128)(2,1)} custom-call(bf16[8,64,512]{2,1,0:T(8,128)(2,1)} %refs_0_.1, s32[8,64]{1,0:T(8,128)} %refs_1_.1, bf16[512,512]{1,0:T(8,128)(2,1)} %refs_2_.1, bf16[40,512]{1,0:T(8,128)(2,1)} %bitcast.10, bf16[40,512]{1,0:T(8,128)(2,1)} %bitcast.11, bf16[512,512]{1,0:T(8,128)(2,1)} %refs_5_.1, bf16[512,512]{1,0:T(8,128)(2,1)} %refs_6_.1, ...), custom_call_target="tpu_custom_call" | custom-call | tf_op jit(solution)/shard_map/pallas_call | solution.py:429
  38.9 1.9 %copy.17 = bf16[8,64,512]{2,1,0:T(8,128)(2,1)} copy(bf16[8,64,512]{2,1,0:T(8,128)(2,1)} %shard_map.145) | data formatting | bytes 1048576

commit v3 on v2

--- a/solution.py
+++ b/solution.py
@@ -8,6 +8,8 @@
 from jax.sharding import PartitionSpec as P
 
 MESH = pl.DeviceIdType.MESH
+GROUPS = 2
+STAGES = 2
 f32 = jnp.float32
 bf16 = jnp.bfloat16
 
@@ -107,6 +109,9 @@
         send_sems,
         recv_sems,
         relay_sems,
+        down_out,
+        down_in,
+        down_sems,
         load_sems,
     ) = refs[2 * count + 1 :]
     loads = {
@@ -139,8 +144,13 @@
     tokens = local_rows * width
     chunk = width
     chunks = tokens // chunk
-    per_peer = width // n_rows
-    height = n_rows * local_rows
+    members = n_rows // GROUPS
+    per_peer = width // members
+    height = members * local_rows
+    stage_tokens = tokens // STAGES
+    stage_chunks = chunks // STAGES
+    stage_lines = per_peer // STAGES
+    per_line = height // chunk
     assert head_width == chunk and height % chunk == 0
 
     my_row = lax.axis_index("rows")
@@ -148,13 +158,23 @@
 
     barrier = pltpu.get_barrier_semaphore()
 
-    @pl.loop(1, n_rows)
+    group_of = my_row // members
+    member = lax.rem(my_row, members)
+    base = group_of * members
+
+    def fellow(off):
+        return lax.rem(member + off, members)
+
+    @pl.loop(1, members)
     def _(off):
         pl.semaphore_signal(
-            barrier,
-            inc=1,
-            device_id=(lax.rem(my_row + off, n_rows), my_col),
-            device_id_type=MESH,
+            barrier, inc=1, device_id=(base + fellow(off), my_col), device_id_type=MESH
+        )
+
+    @pl.when(group_of > 0)
+    def _():
+        pl.semaphore_signal(
+            barrier, inc=1, device_id=(my_row - members, my_col), device_id_type=MESH
         )
 
     @pl.when(my_col > 0)
@@ -170,7 +190,7 @@
     place_u = iota((chunk, feats), 1) & (head_width - 1)
     causal = place_t >= place_u
     diagonal = place_t == place_u
-    pair = 2 if chunks % 2 == 0 else 1
+    pair = 2 if stage_chunks % 2 == 0 else 1
     span = pair * chunk
     tri_t, tri_u = iota((span, span), 0), iota((span, span), 1)
     csh = log2_of(chunk)
@@ -205,20 +225,21 @@
             jnp.concatenate([high, low], axis=0), jnp.concatenate([expand, expand], axis=0)
         )
 
-    def project(x, w_ref, bias, neg_rates):
+    def project(x, w_ref, bias, neg_rates, start=0):
+        here = slice(start, start + x.shape[0])
         weights = w_ref[...]
         proj = mm_nt(x, weights[: 2 * states])
-        b_all[...] = proj[:, :states].astype(bf16)
-        c_all[...] = proj[:, states:].astype(bf16)
+        b_all[here, :] = proj[:, :states].astype(bf16)
+        c_all[here, :] = proj[:, states:].astype(bf16)
         turned = mm_nt(weights, x)
-        bt_all[...] = turned[:states].astype(bf16)
+        bt_all[:, here] = turned[:states].astype(bf16)
         v = turned[2 * states :] + bias
         steps = jnp.maximum(v, 0.0) + jnp.log1p(jnp.exp(-jnp.abs(v)))
-        v_all[...] = (spread(steps) * vals[...].astype(f32)).astype(bf16)
+        v_all[here, :] = (spread(steps) * vals[here, :].astype(f32)).astype(bf16)
         high, low = parts_of(spread(steps * neg_rates))
-        for g in range(0, chunks, pair):
-            rows = slice(g * chunk, (g + pair) * chunk)
-            l_exp[rows, :] = mm(tri, jnp.concatenate([high[rows], low[rows]], axis=0))
+        for g in range(0, x.shape[0], span):
+            rows = slice(g, g + span)
+            l_exp[start + g : start + g + span, :] = mm(tri, jnp.concatenate([high[rows], low[rows]], axis=0))
 
     def push(g):
         rows = slice(g * chunk, (g + 1) * chunk)
@@ -243,47 +264,41 @@
             outs.append(mm(weights[:, lanes], stacked))
         return jnp.concatenate(outs, axis=1) + skips * vals[rows, :].astype(f32)
 
-    def exchange(slot, source, target):
-        def copy_of(off):
-            to = lax.rem(my_row + off, n_rows)
+    def exchange(slot, stage, source, target):
+        source, target = source.at[stage], target.at[stage]
+
+        def copy_of(off, to, place):
             return pltpu.make_async_remote_copy(
                 src_ref=source.at[to],
-                dst_ref=target.at[my_row],
-                send_sem=send_sems.at[slot, off],
-                recv_sem=recv_sems.at[slot, off],
-                device_id=(to, my_col),
+                dst_ref=target.at[place],
+                send_sem=send_sems.at[slot, stage, off],
+                recv_sem=recv_sems.at[slot, stage, off],
+                device_id=(base + to, my_col),
                 device_id_type=MESH,
             )
 
         def start():
-            @pl.loop(1, n_rows)
+            @pl.loop(1, members)
             def _(off):
-                copy_of(off).start()
-
-            target[my_row] = source[my_row]
+                copy_of(off, fellow(off), member).start()
+
+            target[member] = source[member]
 
         def finish():
-            @pl.loop(1, n_rows)
+            @pl.loop(1, members)
             def _(off):
-                came = lax.rem(my_row + n_rows - off, n_rows)
-                pltpu.make_async_remote_copy(
-                    src_ref=source.at[came],
-                    dst_ref=target.at[came],
-                    send_sem=send_sems.at[slot, off],
-                    recv_sem=recv_sems.at[slot, off],
-                    device_id=(came, my_col),
-                    device_id_type=MESH,
-                ).wait_recv()
+                came = fellow(members - off)
+                copy_of(off, came, came).wait_recv()
 
         def drain():
-            @pl.loop(1, n_rows)
+            @pl.loop(1, members)
             def _(off):
-                copy_of(off).wait_send()
+                copy_of(off, fellow(off), member).wait_send()
 
         return start, finish, drain
 
     def put(ref, x):
-        if ref.shape[1] % 16:
+        if ref.shape[-2] % 16:
             x = x.astype(f32).reshape(ref.shape).astype(bf16)
         else:
             x = x.astype(bf16).reshape(ref.shape)
@@ -291,20 +306,26 @@
 
     def take(ref):
         x = ref[...]
-        if ref.shape[1] % 16:
-            return x.astype(f32).reshape(tokens, feats).astype(bf16)
-        return x.reshape(tokens, feats)
+        if ref.shape[-2] % 16:
+            return x.astype(f32).reshape(-1, feats).astype(bf16)
+        return x.reshape(-1, feats)
 
     rsh = log2_of(local_rows)
     hsh = log2_of(height)
-    psh = log2_of(per_peer)
+    lsh = log2_of(stage_lines)
+    msh = log2_of(members)
     m = iota((tokens, 128), 0)
-    by_col = one_hot(((m & (local_rows - 1)) << csh) + lax.shift_right_logical(m, rsh))
+    shr = lax.shift_right_logical
+    by_col = one_hot(
+        ((m & (local_rows - 1)) << csh)
+        + ((shr(m, rsh + lsh) & (members - 1)) << log2_of(per_peer))
+        + (shr(m, rsh + lsh + msh) << lsh)
+        + (shr(m, rsh) & (stage_lines - 1))
+    )
+    m = iota((stage_tokens, 128), 0)
     i_of = m & (height - 1)
     to_columns = one_hot(
-        (lax.shift_right_logical(i_of, rsh) << (rsh + psh))
-        + (lax.shift_right_logical(m, hsh) << rsh)
-        + (i_of & (local_rows - 1))
+        (shr(i_of, rsh) << (rsh + lsh)) + (shr(m, hsh) << rsh) + (i_of & (local_rows - 1))
     )
 
     loads["tissue"].wait()
@@ -326,7 +347,12 @@
     for g in range(chunks):
         l_end[g], pushed_all[g] = push(g)
 
-    greeted = n_rows - 1 + jnp.where(my_col < n_cols - 1, 1, 0)
+    greeted = (
+        members
+        - 1
+        + jnp.where(my_col < n_cols - 1, 1, 0)
+        + jnp.where(group_of < GROUPS - 1, 1, 0)
+    )
     pl.semaphore_wait(barrier, greeted)
 
     relay = pltpu.make_async_remote_copy(
@@ -367,8 +393,9 @@
         vals[rows, :] = (y * scale * gain_a).astype(bf16)
 
     put(send1, mm(by_col, vals[...]))
-    start1, finish1, drain1 = exchange(0, send1, recv1)
-    start1()
+    across = [exchange(0, k, send1, recv1) for k in range(STAGES)]
+    for start, _, _ in across:
+        start()
 
     loads["w_gate"].wait()
     gate = mm(masked[...], w_gate_ref[...])
@@ -382,36 +409,80 @@
     def _():
         relay.wait_send()
 
-    finish1()
-    cols = mm(to_columns, take(recv1)).astype(bf16)
-    vals[...] = cols
-    project(cols, w_down_ref, bias_d, neg_rates_d)
-
-    per_line = height // chunk
-    for c in range(per_peer):
-        entered = None
-        for g in range(c * per_line, (c + 1) * per_line):
-            rows = slice(g * chunk, (g + 1) * chunk)
-            end, pushed = push(g)
-            y = within(g, skips_d)
-            if entered is None:
-                entered = pushed
-            else:
-                y = y + mm(c_all[rows, :], entered.astype(bf16)) * jnp.exp(l_exp[rows, :])
-                entered = jnp.exp(end) * entered + pushed
-            y_all[rows, :] = y
-
-    put(send2, mm_tn(to_columns, y_all[...].astype(bf16)))
-    start2, finish2, drain2 = exchange(1, send2, recv2)
-    start2()
-    drain1()
-    finish2()
+    hand_down = [
+        pltpu.make_async_remote_copy(
+            src_ref=down_out.at[k],
+            dst_ref=down_in.at[k],
+            send_sem=down_sems.at[0, k],
+            recv_sem=down_sems.at[1, k],
+            device_id=(lax.rem(my_row + members, n_rows), my_col),
+            device_id_type=MESH,
+        )
+        for k in range(STAGES)
+    ]
+
+    @pl.when(group_of == 0)
+    def _():
+        down_in[...] = jnp.zeros_like(down_in)
+
+    for k in range(STAGES):
+        across[k][1]()
+        first_token = k * stage_tokens
+        cols = mm(to_columns, take(recv1.at[k])).astype(bf16)
+        vals[first_token : first_token + stage_tokens, :] = cols
+        project(cols, w_down_ref, bias_d, neg_rates_d, first_token)
+        for c in range(stage_lines):
+            entered = None
+            for i in range(per_line):
+                g = k * stage_chunks + c * per_line + i
+                end, pushed = push(g)
+                l_end[g], pushed_all[g] = end, pushed
+                entered = pushed if entered is None else jnp.exp(end) * entered + pushed
+            down_out[k, c] = entered.astype(bf16)
+
+        @pl.when(group_of < GROUPS - 1)
+        def _():
+            hand_down[k].start()
+
+    back = [exchange(1, k, send2, recv2) for k in range(STAGES)]
+    for k in range(STAGES):
+        for g in range(k * stage_chunks, (k + 1) * stage_chunks):
+            y_all[g * chunk : (g + 1) * chunk, :] = within(g, skips_d)
+
+        @pl.when(group_of > 0)
+        def _():
+            hand_down[k].wait_recv()
+
+        parts = []
+        for c in range(stage_lines):
+            entered = down_in[k, c].astype(f32)
+            for i in range(per_line):
+                g = k * stage_chunks + c * per_line + i
+                rows = slice(g * chunk, (g + 1) * chunk)
+                extra = mm(c_all[rows, :], entered.astype(bf16)) * jnp.exp(l_exp[rows, :])
+                parts.append((y_all[rows, :] + extra).astype(bf16))
+                if i < per_line - 1:
+                    entered = jnp.exp(l_end[g]) * entered + pushed_all[g]
+        put(send2.at[k], mm_tn(to_columns, jnp.concatenate(parts, axis=0)))
+        back[k][0]()
+
+    for _, _, drain in across:
+        drain()
+
+    @pl.when(group_of < GROUPS - 1)
+    def _():
+        for copy in hand_down:
+            copy.wait_send()
+
+    for _, finish, _ in back:
+        finish()
     z = mm_tn(by_col, take(recv2))
     scale = lax.rsqrt(jnp.mean(z * z, axis=-1, keepdims=True) + 1e-5)
     act = (z * scale * gated[...]).astype(bf16)
     mixed = masked[...].astype(f32) + mm(act, w_out_ref[...])
     out_ref[...] = mixed.astype(bf16).reshape(out_ref.shape)
-    drain2()
+    for _, _, drain in back:
+        drain()
 
 
 def on_device(n_rows, n_cols, *args):
@@ -423,7 +494,10 @@
     heads = args[9].shape[1]
     states = (args[3].shape[0] - heads) // 2
     chunks = local_rows
-    piece = (n_rows, local_rows * (width // n_rows), feats)
+    members = n_rows // GROUPS
+    stage_lines = width // members // STAGES
+    piece = (STAGES, members, local_rows * stage_lines, feats)
+    down = (STAGES, stage_lines, states, feats)
     big = (tokens, feats)
     vmem = pl.BlockSpec(memory_space=pltpu.VMEM)
     return pl.pallas_call(
@@ -450,9 +524,12 @@
             pltpu.VMEM(piece, bf16),
             pltpu.VMEM(piece, bf16),
             pltpu.VMEM(piece, bf16),
-            pltpu.SemaphoreType.DMA((2, n_rows)),
-            pltpu.SemaphoreType.DMA((2, n_rows)),
+            pltpu.SemaphoreType.DMA((2, STAGES, members)),
+            pltpu.SemaphoreType.DMA((2, STAGES, members)),
             pltpu.SemaphoreType.DMA((2,)),
+            pltpu.VMEM(down, bf16),
+            pltpu.VMEM(down, bf16),
+            pltpu.SemaphoreType.DMA((2, STAGES)),
             pltpu.SemaphoreType.DMA((len(args),)),
         ],
         compiler_params=pltpu.CompilerParams(

time: 40.9 us -> 32.8 us (0.80)
  the two profiles are of different devices: /device:TPU:27 before, /device:TPU:23 now
where the time goes in v3:
time: 32.8 us; the launch traced here: 32.7 us
  Pallas kernels  30.8 us (94%)
  local copies, waits for them, and re-layouts  1.87 us (6%)
    pallas_call x1, Pallas kernels, on_device(): pl.pallas_call(functools.partial(block_kernel, n_rows, n_cols), out_shape...  30.8 us
    unnamed x1, local copies, waits for them, and re-layouts  1.87 us

profile of v3, /device:TPU:23, one launch (start us, length us, event | category | flops | bytes accessed | tf_op | source)
XLA Modules:
  0.0 32.7 jit_solution(7649286831520936465)
XLA Ops:
  0.0 30.8 %shard_map.145 = bf16[8,64,512]{2,1,0:T(8,128)(2,1)} custom-call(bf16[8,64,512]{2,1,0:T(8,128)(2,1)} %refs_0_.1, s32[8,64]{1,0:T(8,128)} %refs_1_.1, bf16[512,512]{1,0:T(8,128)(2,1)} %refs_2_.1, bf16[40,512]{1,0:T(8,128)(2,1)} %bitcast.10, bf16[40,512]{1,0:T(8,128)(2,1)} %bitcast.11, bf16[512,512]{1,0:T(8,128)(2,1)} %refs_5_.1, bf16[512,512]{1,0:T(8,128)(2,1)} %refs_6_.1, ...), custom_call_target="tpu_custom_call" | custom-call | tf_op jit(solution)/shard_map/pallas_call | solution.py:503
  30.8 1.9 %copy.17 = bf16[8,64,512]{2,1,0:T(8,128)(2,1)} copy(bf16[8,64,512]{2,1,0:T(8,128)(2,1)} %shard_map.145) | data formatting | bytes 1048576

commit v4 on v3

--- a/solution.py
+++ b/solution.py
@@ -10,6 +10,7 @@
 MESH = pl.DeviceIdType.MESH
 GROUPS = 2
 STAGES = 2
+HALVES = 2
 f32 = jnp.float32
 bf16 = jnp.bfloat16
 
@@ -98,6 +99,8 @@
         l_exp,
         y_all,
         gated,
+        ordered,
+        mixed_all,
         pushed_all,
         l_end,
         state_out,
@@ -149,6 +152,8 @@
     height = members * local_rows
     stage_tokens = tokens // STAGES
     stage_chunks = chunks // STAGES
+    half_rows = local_rows // HALVES
+    half_tokens = tokens // HALVES
     stage_lines = per_peer // STAGES
     per_line = height // chunk
     assert head_width == chunk and height % chunk == 0
@@ -264,15 +269,13 @@
             outs.append(mm(weights[:, lanes], stacked))
         return jnp.concatenate(outs, axis=1) + skips * vals[rows, :].astype(f32)
 
-    def exchange(slot, stage, source, target):
-        source, target = source.at[stage], target.at[stage]
-
+    def exchange(source, target, sems, part):
         def copy_of(off, to, place):
             return pltpu.make_async_remote_copy(
-                src_ref=source.at[to],
-                dst_ref=target.at[place],
-                send_sem=send_sems.at[slot, stage, off],
-                recv_sem=recv_sems.at[slot, stage, off],
+                src_ref=source.at[(to,) + part],
+                dst_ref=target.at[(place,) + part],
+                send_sem=send_sems.at[sems, off],
+                recv_sem=recv_sems.at[sems, off],
                 device_id=(base + to, my_col),
                 device_id_type=MESH,
             )
@@ -282,7 +285,7 @@
             def _(off):
                 copy_of(off, fellow(off), member).start()
 
-            target[member] = source[member]
+            target[(member,) + part] = source[(member,) + part]
 
         def finish():
             @pl.loop(1, members)
@@ -297,27 +300,24 @@
 
         return start, finish, drain
 
-    def put(ref, x):
-        if ref.shape[-2] % 16:
-            x = x.astype(f32).reshape(ref.shape).astype(bf16)
-        else:
-            x = x.astype(bf16).reshape(ref.shape)
-        ref[...] = x
-
-    def take(ref):
-        x = ref[...]
-        if ref.shape[-2] % 16:
+    def shaped(x, shape):
+        if shape[-2] % 16:
+            return x.astype(f32).reshape(shape).astype(bf16)
+        return x.astype(bf16).reshape(shape)
+
+    def flat(x):
+        if x.shape[-2] % 16:
             return x.astype(f32).reshape(-1, feats).astype(bf16)
         return x.reshape(-1, feats)
 
-    rsh = log2_of(local_rows)
+    rsh = log2_of(half_rows)
     hsh = log2_of(height)
     lsh = log2_of(stage_lines)
     msh = log2_of(members)
-    m = iota((tokens, 128), 0)
     shr = lax.shift_right_logical
+    m = iota((half_tokens, 128), 0)
     by_col = one_hot(
-        ((m & (local_rows - 1)) << csh)
+        ((m & (half_rows - 1)) << csh)
         + ((shr(m, rsh + lsh) & (members - 1)) << log2_of(per_peer))
         + (shr(m, rsh + lsh + msh) << lsh)
         + (shr(m, rsh) & (stage_lines - 1))
@@ -325,8 +325,15 @@
     m = iota((stage_tokens, 128), 0)
     i_of = m & (height - 1)
     to_columns = one_hot(
-        (shr(i_of, rsh) << (rsh + lsh)) + (shr(m, hsh) << rsh) + (i_of & (local_rows - 1))
+        (shr(i_of, rsh) << (rsh + lsh)) + (shr(m, hsh) << rsh) + (i_of & (half_rows - 1))
     )
+
+    def half(h):
+        return slice(h * half_tokens, (h + 1) * half_tokens)
+
+    def out_order(ref, h, x):
+        x = mm(by_col, x)
+        ref[:, :, h] = shaped(x, (STAGES, members) + ref.shape[3:])
 
     loads["tissue"].wait()
     loads["patches"].wait()
@@ -344,8 +351,25 @@
     project(x, w_across_ref, tall(bias_a_ref), -tall(rates_a_ref))
     skips = wide(skip_a_ref)
 
-    for g in range(chunks):
-        l_end[g], pushed_all[g] = push(g)
+    relays = [
+        pltpu.make_async_remote_copy(
+            src_ref=state_out.at[pl.ds(h * half_rows, half_rows)],
+            dst_ref=state_in.at[pl.ds(h * half_rows, half_rows)],
+            send_sem=relay_sems.at[0, h],
+            recv_sem=relay_sems.at[1, h],
+            device_id=(my_row, lax.rem(my_col + 1, n_cols)),
+            device_id_type=MESH,
+        )
+        for h in range(HALVES)
+    ]
+
+    def rows_of(h):
+        return range(h * half_rows, (h + 1) * half_rows)
+
+    @pl.when(my_col < n_cols - 1)
+    def _():
+        for g in range(chunks):
+            l_end[g], pushed_all[g] = push(g)
 
     greeted = (
         members
@@ -355,51 +379,55 @@
     )
     pl.semaphore_wait(barrier, greeted)
 
-    relay = pltpu.make_async_remote_copy(
-        src_ref=state_out,
-        dst_ref=state_in,
-        send_sem=relay_sems.at[0],
-        recv_sem=relay_sems.at[1],
-        device_id=(my_row, lax.rem(my_col + 1, n_cols)),
-        device_id_type=MESH,
-    )
-
     @pl.when(my_col == 0)
     def _():
         state_in[...] = jnp.zeros_like(state_in)
         if n_cols > 1:
-            state_out[...] = pushed_all[...].astype(bf16)
-            relay.start()
+            for h in range(HALVES):
+                for g in rows_of(h):
+                    state_out[g] = pushed_all[g].astype(bf16)
+                relays[h].start()
 
     for g in range(chunks):
         y_all[g * chunk : (g + 1) * chunk, :] = within(g, skips)
 
-    @pl.when(my_col > 0)
-    def _():
-        relay.wait_recv()
-
-        @pl.when(my_col < n_cols - 1)
+    gain_a = gain_a_ref[...]
+    across = [
+        [exchange(send1.at[k], recv1.at[k], k * HALVES + h, (h,)) for k in range(STAGES)]
+        for h in range(HALVES)
+    ]
+    for h in range(HALVES):
+
+        @pl.when(my_col > 0)
         def _():
-            state_out[...] = (
-                pushed_all[...] + jnp.exp(l_end[...]) * state_in[...].astype(f32)
-            ).astype(bf16)
-            relay.start()
-
-    gain_a = gain_a_ref[...]
-    for g in range(chunks):
-        rows = slice(g * chunk, (g + 1) * chunk)
-        y = y_all[rows, :] + mm(c_all[rows, :], state_in[g]) * jnp.exp(l_exp[rows, :])
-        scale = lax.rsqrt(jnp.mean(y * y, axis=-1, keepdims=True) + 1e-5)
-        vals[rows, :] = (y * scale * gain_a).astype(bf16)
-
-    put(send1, mm(by_col, vals[...]))
-    across = [exchange(0, k, send1, recv1) for k in range(STAGES)]
-    for start, _, _ in across:
-        start()
-
+            relays[h].wait_recv()
+
+            @pl.when(my_col < n_cols - 1)
+            def _():
+                for g in rows_of(h):
+                    state_out[g] = (
+                        pushed_all[g] + jnp.exp(l_end[g]) * state_in[g].astype(f32)
+                    ).astype(bf16)
+                relays[h].start()
+
+        parts = []
+        for g in rows_of(h):
+            rows = slice(g * chunk, (g + 1) * chunk)
+            y = y_all[rows, :] + mm(c_all[rows, :], state_in[g]) * jnp.exp(l_exp[rows, :])
+            scale = lax.rsqrt(jnp.mean(y * y, axis=-1, keepdims=True) + 1e-5)
+            parts.append((y * scale * gain_a).astype(bf16))
+        out_order(send1, h, jnp.concatenate(parts, axis=0))
+        for k in range(STAGES):
+            across[h][k][0]()
+
+    for h in range(HALVES):
+        out_order(ordered, h, masked[half(h), :])
     loads["w_gate"].wait()
-    gate = mm(masked[...], w_gate_ref[...])
-    gated[...] = gate / (1.0 + jnp.exp(-gate)) * gain_f_ref[...]
+    for k in range(STAGES):
+        gate = mm(flat(ordered[k]), w_gate_ref[...])
+        gated[k * stage_tokens : (k + 1) * stage_tokens, :] = (
+            gate / (1.0 + jnp.exp(-gate)) * gain_f_ref[...]
+        )
     skips_d = wide(skip_d_ref)
     bias_d, neg_rates_d = tall(bias_d_ref), -tall(rates_d_ref)
     loads["w_down"].wait()
@@ -407,7 +435,8 @@
 
     @pl.when(my_col < n_cols - 1)
     def _():
-        relay.wait_send()
+        for copy in relays:
+            copy.wait_send()
 
     hand_down = [
         pltpu.make_async_remote_copy(
@@ -425,29 +454,38 @@
     def _():
         down_in[...] = jnp.zeros_like(down_in)
 
-    for k in range(STAGES):
-        across[k][1]()
-        first_token = k * stage_tokens
-        cols = mm(to_columns, take(recv1.at[k])).astype(bf16)
-        vals[first_token : first_token + stage_tokens, :] = cols
-        project(cols, w_down_ref, bias_d, neg_rates_d, first_token)
+    def ends(k):
         for c in range(stage_lines):
             entered = None
             for i in range(per_line):
                 g = k * stage_chunks + c * per_line + i
                 end, pushed = push(g)
-                l_end[g], pushed_all[g] = end, pushed
+                if per_line > 1:
+                    l_end[g], pushed_all[g] = end, pushed
                 entered = pushed if entered is None else jnp.exp(end) * entered + pushed
             down_out[k, c] = entered.astype(bf16)
 
+    for k in range(STAGES):
+        for h in range(HALVES):
+            across[h][k][1]()
+        first_token = k * stage_tokens
+        cols = mm(to_columns, flat(recv1[k])).astype(bf16)
+        vals[first_token : first_token + stage_tokens, :] = cols
+        project(cols, w_down_ref, bias_d, neg_rates_d, first_token)
+        if per_line > 1:
+            ends(k)
+
         @pl.when(group_of < GROUPS - 1)
         def _():
+            if per_line == 1:
+                ends(k)
             hand_down[k].start()
 
-    back = [exchange(1, k, send2, recv2) for k in range(STAGES)]
-    for k in range(STAGES):
         for g in range(k * stage_chunks, (k + 1) * stage_chunks):
             y_all[g * chunk : (g + 1) * chunk, :] = within(g, skips_d)
+
+    back = [exchange(send2.at[k], recv2.at[k], STAGES * HALVES + k, ()) for k in range(STAGES)]
+    for k in range(STAGES):
 
         @pl.when(group_of > 0)
         def _():
@@ -463,24 +501,29 @@
                 parts.append((y_all[rows, :] + extra).astype(bf16))
                 if i < per_line - 1:
                     entered = jnp.exp(l_end[g]) * entered + pushed_all[g]
-        put(send2.at[k], mm_tn(to_columns, jnp.concatenate(parts, axis=0)))
+        send2[k] = shaped(mm_tn(to_columns, jnp.concatenate(parts, axis=0)), send2.shape[1:])
         back[k][0]()
 
-    for _, _, drain in across:
-        drain()
+    for k in range(STAGES):
+        back[k][1]()
+        z = flat(recv2[k]).astype(f32)
+        scale = lax.rsqrt(jnp.mean(z * z, axis=-1, keepdims=True) + 1e-5)
+        act = z * scale * gated[k * stage_tokens : (k + 1) * stage_tokens, :]
+        mixed = flat(ordered[k]).astype(f32) + mm(act.astype(bf16), w_out_ref[...])
+        mixed_all[k] = shaped(mixed, mixed_all.shape[1:])
+    for h in range(HALVES):
+        mixed = mm_tn(by_col, flat(mixed_all[:, :, h])).astype(bf16)
+        out_ref[h * half_rows : (h + 1) * half_rows] = mixed.reshape(half_rows, width, feats)
+
+    for h in range(HALVES):
+        for k in range(STAGES):
+            across[h][k][2]()
 
     @pl.when(group_of < GROUPS - 1)
     def _():
         for copy in hand_down:
             copy.wait_send()
 
-    for _, finish, _ in back:
-        finish()
-    z = mm_tn(by_col, take(recv2))
-    scale = lax.rsqrt(jnp.mean(z * z, axis=-1, keepdims=True) + 1e-5)
-    act = (z * scale * gated[...]).astype(bf16)
-    mixed = masked[...].astype(f32) + mm(act, w_out_ref[...])
-    out_ref[...] = mixed.astype(bf16).reshape(out_ref.shape)
     for _, _, drain in back:
         drain()
 
@@ -496,14 +539,14 @@
     chunks = local_rows
     members = n_rows // GROUPS
     stage_lines = width // members // STAGES
-    piece = (STAGES, members, local_rows * stage_lines, feats)
+    piece = (STAGES, members, HALVES, local_rows // HALVES * stage_lines, feats)
     down = (STAGES, stage_lines, states, feats)
     big = (tokens, feats)
     vmem = pl.BlockSpec(memory_space=pltpu.VMEM)
     return pl.pallas_call(
         functools.partial(block_kernel, n_rows, n_cols),
         out_shape=jax.ShapeDtypeStruct(patches.shape, bf16),
-        in_specs=[pl.BlockSpec(memory_space=pl.ANY)] * len(args),
+        in_specs=[pl.BlockSpec(memory_space=pltpu.HBM)] * len(args),
         out_specs=vmem,
         scratch_shapes=[pltpu.VMEM(a.shape, a.dtype) for a in args]
         + [
@@ -516,6 +559,8 @@
             pltpu.VMEM(big, f32),
             pltpu.VMEM(big, f32),
             pltpu.VMEM(big, f32),
+            pltpu.VMEM(piece, bf16),
+            pltpu.VMEM(piece, bf16),
             pltpu.VMEM((chunks, states, feats), f32),
             pltpu.VMEM((chunks, 1, feats), f32),
             pltpu.VMEM((chunks, states, feats), bf16),
@@ -524,16 +569,16 @@
             pltpu.VMEM(piece, bf16),
             pltpu.VMEM(piece, bf16),
             pltpu.VMEM(piece, bf16),
-            pltpu.SemaphoreType.DMA((2, STAGES, members)),
-            pltpu.SemaphoreType.DMA((2, STAGES, members)),
-            pltpu.SemaphoreType.DMA((2,)),
+            pltpu.SemaphoreType.DMA((STAGES * (HALVES + 1), members)),
+            pltpu.SemaphoreType.DMA((STAGES * (HALVES + 1), members)),
+            pltpu.SemaphoreType.DMA((2, HALVES)),
             pltpu.VMEM(down, bf16),
             pltpu.VMEM(down, bf16),
             pltpu.SemaphoreType.DMA((2, STAGES)),
             pltpu.SemaphoreType.DMA((len(args),)),
         ],
         compiler_params=pltpu.CompilerParams(
-            collective_id=0, has_side_effects=True, vmem_limit_bytes=56 * 1024 * 1024
+            collective_id=0, has_side_effects=True, vmem_limit_bytes=32 * 1024 * 1024
         ),
     )(*args)
 

time: 32.8 us -> 36.7 us (1.12)
  local copies, waits for them, and re-layouts: 1.87 us -> 7.24 us
  Pallas kernels: 30.8 us -> 28.9 us
    unnamed x1 -> x31, local copies, waits for them, and re-layouts: 1.87 us -> 7.24 us
    pallas_call x1, Pallas kernels: 30.8 us -> 28.9 us  [on_device(): pl.pallas_call(functools.partial(block_kernel, n_rows, n_cols), out_shape...]
where the time goes in v4:
time: 36.7 us; the launch traced here: 36.2 us
  Pallas kernels  28.9 us (79%)
  local copies, waits for them, and re-layouts  7.24 us (20%)
    pallas_call x1, Pallas kernels, on_device(): pl.pallas_call(functools.partial(block_kernel, n_rows, n_cols), out_shape...  28.9 us
    unnamed x31, local copies, waits for them, and re-layouts  7.24 us

profile of v4, /device:TPU:23, one launch (start us, length us, event | category | flops | bytes accessed | tf_op | source)
XLA Modules:
  0.0 36.2 jit_solution(15447309725033154382)
XLA Ops:
  0.0 0.0 copy-start.11
  0.0 0.0 copy-start.12
  0.0 0.0 copy-start.13
  0.0 0.0 copy-start.14
  0.0 0.0 copy-start.8
  0.0 0.0 copy-start.6
  0.0 0.0 copy-start.7
  0.0 0.0 copy-start.9
  0.1 0.0 copy-start.10
  0.1 0.6 %copy-done.11 = f32[8]{0:T(128)S(1)} copy-done((f32[8]{0:T(128)S(1)}, f32[8]{0:T(128)}, u32[]{:S(2)}) %copy-start.11) | copy-done | bytes 56
  0.7 0.0 copy-done.12
  0.7 0.0 copy-done.13
  0.7 0.0 copy-done.14
  0.7 0.0 copy-done.8
  0.7 0.0 copy-done.6
  0.8 0.0 copy-done.7
  0.8 0.0 copy-done.9
  0.8 0.0 copy-done.10
  0.8 0.0 copy-start
  0.8 1.0 %copy-done = bf16[8,64,512]{2,1,0:T(8,128)(2,1)S(1)} copy-done((bf16[8,64,512]{2,1,0:T(8,128)(2,1)S(1)}, bf16[8,64,512]{2,1,0:T(8,128)(2,1)}, u32[]{:S(2)}) %copy-start) | copy-done | bytes 524312
  1.8 0.0 copy-start.1
  1.8 1.0 %copy-done.1 = bf16[512,512]{1,0:T(8,128)(2,1)S(1)} copy-done((bf16[512,512]{1,0:T(8,128)(2,1)S(1)}, bf16[512,512]{1,0:T(8,128)(2,1)}, u32[]{:S(2)}) %copy-start.1) | copy-done | bytes 524312
  2.9 0.0 copy-start.2
  2.9 1.0 %copy-done.2 = bf16[512,512]{1,0:T(8,128)(2,1)S(1)} copy-done((bf16[512,512]{1,0:T(8,128)(2,1)S(1)}, bf16[512,512]{1,0:T(8,128)(2,1)}, u32[]{:S(2)}) %copy-start.2) | copy-done | bytes 524312
  3.9 0.0 copy-start.3
  3.9 1.0 %copy-done.3 = bf16[512,512]{1,0:T(8,128)(2,1)S(1)} copy-done((bf16[512,512]{1,0:T(8,128)(2,1)S(1)}, bf16[512,512]{1,0:T(8,128)(2,1)}, u32[]{:S(2)}) %copy-start.3) | copy-done | bytes 524312
  5.0 0.0 copy-start.4
  5.0 0.8 %copy-done.4 = bf16[512,40]{0,1:T(8,128)(2,1)S(1)} copy-done((bf16[512,40]{0,1:T(8,128)(2,1)S(1)}, bf16[512,40]{0,1:T(8,128)(2,1)}, u32[]{:S(2)}) %copy-start.4) | copy-done | bytes 40984
  5.7 0.0 copy-start.5
  5.7 0.8 %copy-done.5 = bf16[512,40]{0,1:T(8,128)(2,1)S(1)} copy-done((bf16[512,40]{0,1:T(8,128)(2,1)S(1)}, bf16[512,40]{0,1:T(8,128)(2,1)}, u32[]{:S(2)}) %copy-start.5) | copy-done | bytes 40984
  6.5 28.9 %shard_map.145 = bf16[8,64,512]{2,1,0:T(8,128)(2,1)S(1)} custom-call(bf16[8,64,512]{2,1,0:T(8,128)(2,1)S(1)} %copy-done, s32[8,64]{1,0:T(8,128)S(1)} %copy-done.6, bf16[512,512]{1,0:T(8,128)(2,1)S(1)} %copy-done.1, bf16[40,512]{1,0:T(8,128)(2,1)S(1)} %bitcast.10, bf16[40,512]{1,0:T(8,128)(2,1)S(1)} %bitcast.11, bf16[512,512]{1,0:T(8,128)(2,1)S(1)} %copy-done.2, ...), custom_call_target="tpu_custom_call" | custom-call | tf_op jit(solution)/shard_map/pallas_call | solution.py:546
  35.4 0.8 %copy.17 = bf16[8,64,512]{2,1,0:T(8,128)(2,1)} copy(bf16[8,64,512]{2,1,0:T(8,128)(2,1)S(1)} %shard_map.145) | data formatting | bytes 1048576
Async XLA Ops:
  0.0 0.7 %copy-start.11 = (f32[8]{0:T(128)S(1)}, f32[8]{0:T(128)}, u32[]{:S(2)}) copy-start(f32[8]{0:T(128)} %param.24) | copy-start | bytes 100
  0.0 0.7 %copy-start.12 = (f32[8]{0:T(128)S(1)}, f32[8]{0:T(128)}, u32[]{:S(2)}) copy-start(f32[8]{0:T(128)} %param.25) | copy-start | bytes 100
  0.0 0.7 %copy-start.13 = (f32[8]{0:T(128)S(1)}, f32[8]{0:T(128)}, u32[]{:S(2)}) copy-start(f32[8]{0:T(128)} %param.26) | copy-start | bytes 100
  0.0 0.7 %copy-start.14 = (f32[8]{0:T(128)S(1)}, f32[8]{0:T(128)}, u32[]{:S(2)}) copy-start(f32[8]{0:T(128)} %param.27) | copy-start | bytes 100
  0.0 0.7 %copy-start.8 = (f32[512]{0:T(512)S(1)}, f32[512]{0:T(512)}, u32[]{:S(2)}) copy-start(f32[512]{0:T(512)} %param.29) | copy-start | bytes 6148
  0.0 0.7 %copy-start.6 = (s32[8,64]{1,0:T(8,128)S(1)}, s32[8,64]{1,0:T(8,128)}, u32[]{:S(2)}) copy-start(s32[8,64]{1,0:T(8,128)} %refs_1_.1) | copy-start | bytes 6148
  0.0 0.7 %copy-start.7 = (f32[512]{0:T(512)S(1)}, f32[512]{0:T(512)}, u32[]{:S(2)}) copy-start(f32[512]{0:T(512)} %param.28) | copy-start | bytes 6148
  0.0 0.7 %copy-start.9 = (f32[8]{0:T(128)S(1)}, f32[8]{0:T(128)}, u32[]{:S(2)}) copy-start(f32[8]{0:T(128)} %param.22) | copy-start | bytes 100
  0.1 0.7 %copy-start.10 = (f32[8]{0:T(128)S(1)}, f32[8]{0:T(128)}, u32[]{:S(2)}) copy-start(f32[8]{0:T(128)} %param.23) | copy-start | bytes 100
  0.8 1.0 %copy-start = (bf16[8,64,512]{2,1,0:T(8,128)(2,1)S(1)}, bf16[8,64,512]{2,1,0:T(8,128)(2,1)}, u32[]{:S(2)}) copy-start(bf16[8,64,512]{2,1,0:T(8,128)(2,1)} %refs_0_.1) | copy-start | bytes 1572868
  1.8 1.0 %copy-start.1 = (bf16[512,512]{1,0:T(8,128)(2,1)S(1)}, bf16[512,512]{1,0:T(8,128)(2,1)}, u32[]{:S(2)}) copy-start(bf16[512,512]{1,0:T(8,128)(2,1)} %refs_2_.1) | copy-start | bytes 1572868
  2.9 1.0 %copy-start.2 = (bf16[512,512]{1,0:T(8,128)(2,1)S(1)}, bf16[512,512]{1,0:T(8,128)(2,1)}, u32[]{:S(2)}) copy-start(bf16[512,512]{1,0:T(8,128)(2,1)} %refs_5_.1) | copy-start | bytes 1572868
  3.9 1.0 %copy-start.3 = (bf16[512,512]{1,0:T(8,128)(2,1)S(1)}, bf16[512,512]{1,0:T(8,128)(2,1)}, u32[]{:S(2)}) copy-start(bf16[512,512]{1,0:T(8,128)(2,1)} %refs_6_.1) | copy-start | bytes 1572868
  5.0 0.8 %copy-start.4 = (bf16[512,40]{0,1:T(8,128)(2,1)S(1)}, bf16[512,40]{0,1:T(8,128)(2,1)}, u32[]{:S(2)}) copy-start(bf16[512,40]{0,1:T(8,128)(2,1)} %param.18) | copy-start | bytes 122884
  5.7 0.8 %copy-start.5 = (bf16[512,40]{0,1:T(8,128)(2,1)S(1)}, bf16[512,40]{0,1:T(8,128)(2,1)}, u32[]{:S(2)}) copy-start(bf16[512,40]{0,1:T(8,128)(2,1)} %param.19) | copy-start | bytes 122884

commit v5 on v4

--- a/solution.py
+++ b/solution.py
@@ -9,7 +9,7 @@
 
 MESH = pl.DeviceIdType.MESH
 GROUPS = 2
-STAGES = 2
+MOST_STAGES = 2
 HALVES = 2
 f32 = jnp.float32
 bf16 = jnp.bfloat16
@@ -120,9 +120,23 @@
     loads = {
         name: pltpu.make_async_copy(sources[k], held[k], load_sems.at[k])
         for k, name in enumerate(ARGS)
+        if name != "patches"
     }
+    half_rows = sources[0].shape[0] // HALVES
+    patch_loads = [
+        pltpu.make_async_copy(
+            sources[0].at[pl.ds(h * half_rows, half_rows)],
+            held[0].at[pl.ds(h * half_rows, half_rows)],
+            load_sems.at[count + h],
+        )
+        for h in range(HALVES)
+    ]
     for name in LOAD_ORDER:
-        loads[name].start()
+        if name == "patches":
+            for load in patch_loads:
+                load.start()
+        else:
+            loads[name].start()
     (
         patches_ref,
         tissue_ref,
@@ -150,11 +164,11 @@
     members = n_rows // GROUPS
     per_peer = width // members
     height = members * local_rows
-    stage_tokens = tokens // STAGES
-    stage_chunks = chunks // STAGES
-    half_rows = local_rows // HALVES
+    stages = min(MOST_STAGES, per_peer)
+    stage_tokens = tokens // stages
+    stage_chunks = chunks // stages
     half_tokens = tokens // HALVES
-    stage_lines = per_peer // STAGES
+    stage_lines = per_peer // stages
     per_line = height // chunk
     assert head_width == chunk and height % chunk == 0
 
@@ -170,7 +184,14 @@
     def fellow(off):
         return lax.rem(member + off, members)
 
-    @pl.loop(1, members)
+    def each_fellow(body):
+        if members <= 8:
+            for off in range(1, members):
+                body(off)
+        else:
+            pl.loop(1, members)(body)
+
+    @each_fellow
     def _(off):
         pl.semaphore_signal(
             barrier, inc=1, device_id=(base + fellow(off), my_col), device_id_type=MESH
@@ -281,20 +302,20 @@
             )
 
         def start():
-            @pl.loop(1, members)
+            @each_fellow
             def _(off):
                 copy_of(off, fellow(off), member).start()
 
             target[(member,) + part] = source[(member,) + part]
 
         def finish():
-            @pl.loop(1, members)
+            @each_fellow
             def _(off):
                 came = fellow(members - off)
                 copy_of(off, came, came).wait_recv()
 
         def drain():
-            @pl.loop(1, members)
+            @each_fellow
             def _(off):
                 copy_of(off, fellow(off), member).wait_send()
 
@@ -333,24 +354,13 @@
 
     def out_order(ref, h, x):
         x = mm(by_col, x)
-        ref[:, :, h] = shaped(x, (STAGES, members) + ref.shape[3:])
+        ref[:, :, h] = shaped(x, (stages, members) + ref.shape[3:])
 
     loads["tissue"].wait()
-    loads["patches"].wait()
     flags = tissue_ref[...].astype(f32).T
-    for r in range(local_rows):
-        flag = jnp.broadcast_to(flags[:, r : r + 1], (width, feats)) > 0.5
-        masked[r * width : (r + 1) * width, :] = jnp.where(
-            flag, patches_ref[r].astype(f32), 0.0
-        ).astype(bf16)
-
     for name in ("w_value", "w_across") + SMALL:
         loads[name].wait()
-    x = masked[...]
-    vals[...] = mm(x, w_value_ref[...]).astype(bf16)
-    project(x, w_across_ref, tall(bias_a_ref), -tall(rates_a_ref))
-    skips = wide(skip_a_ref)
-
+    bias_a, neg_rates_a = tall(bias_a_ref), -tall(rates_a_ref)
     relays = [
         pltpu.make_async_remote_copy(
             src_ref=state_out.at[pl.ds(h * half_rows, half_rows)],
@@ -366,34 +376,62 @@
     def rows_of(h):
         return range(h * half_rows, (h + 1) * half_rows)
 
-    @pl.when(my_col < n_cols - 1)
-    def _():
-        for g in range(chunks):
-            l_end[g], pushed_all[g] = push(g)
-
     greeted = (
         members
         - 1
         + jnp.where(my_col < n_cols - 1, 1, 0)
         + jnp.where(group_of < GROUPS - 1, 1, 0)
     )
-    pl.semaphore_wait(barrier, greeted)
 
     @pl.when(my_col == 0)
     def _():
         state_in[...] = jnp.zeros_like(state_in)
+
+    for h in range(HALVES):
+        patch_loads[h].wait()
+        for r in rows_of(h):
+            flag = jnp.broadcast_to(flags[:, r : r + 1], (width, feats)) > 0.5
+            masked[r * width : (r + 1) * width, :] = jnp.where(
+                flag, patches_ref[r].astype(f32), 0.0
+            ).astype(bf16)
+        x = masked[half(h), :]
+        vals[half(h), :] = mm(x, w_value_ref[...]).astype(bf16)
+        project(x, w_across_ref, bias_a, neg_rates_a, h * half_tokens)
+
+        @pl.when(my_col < n_cols - 1)
+        def _():
+            for g in rows_of(h):
+                end, pushed = push(g)
+                state_out[g] = pushed.astype(bf16)
+                if n_cols > 2:
+                    l_end[g], pushed_all[g] = end, pushed
+
+        if h == 0:
+            pl.semaphore_wait(barrier, greeted)
+
         if n_cols > 1:
-            for h in range(HALVES):
-                for g in rows_of(h):
-                    state_out[g] = pushed_all[g].astype(bf16)
+
+            @pl.when(my_col == 0)
+            def _():
                 relays[h].start()
+
+    skips = wide(skip_a_ref)
 
     for g in range(chunks):
         y_all[g * chunk : (g + 1) * chunk, :] = within(g, skips)
 
+    def pass_on(h):
+        @pl.when(my_col < n_cols - 1)
+        def _():
+            for g in rows_of(h):
+                state_out[g] = (
+                    pushed_all[g] + jnp.exp(l_end[g]) * state_in[g].astype(f32)
+                ).astype(bf16)
+            relays[h].start()
+
     gain_a = gain_a_ref[...]
     across = [
-        [exchange(send1.at[k], recv1.at[k], k * HALVES + h, (h,)) for k in range(STAGES)]
+        [exchange(send1.at[k], recv1.at[k], k * HALVES + h, (h,)) for k in range(stages)]
         for h in range(HALVES)
     ]
     for h in range(HALVES):
@@ -402,13 +440,8 @@
         def _():
             relays[h].wait_recv()
 
-            @pl.when(my_col < n_cols - 1)
-            def _():
-                for g in rows_of(h):
-                    state_out[g] = (
-                        pushed_all[g] + jnp.exp(l_end[g]) * state_in[g].astype(f32)
-                    ).astype(bf16)
-                relays[h].start()
+            if n_cols > 2:
+                pass_on(h)
 
         parts = []
         for g in rows_of(h):
@@ -417,13 +450,13 @@
             scale = lax.rsqrt(jnp.mean(y * y, axis=-1, keepdims=True) + 1e-5)
             parts.append((y * scale * gain_a).astype(bf16))
         out_order(send1, h, jnp.concatenate(parts, axis=0))
-        for k in range(STAGES):
+        for k in range(stages):
             across[h][k][0]()
 
     for h in range(HALVES):
         out_order(ordered, h, masked[half(h), :])
     loads["w_gate"].wait()
-    for k in range(STAGES):
+    for k in range(stages):
         gate = mm(flat(ordered[k]), w_gate_ref[...])
         gated[k * stage_tokens : (k + 1) * stage_tokens, :] = (
             gate / (1.0 + jnp.exp(-gate)) * gain_f_ref[...]
@@ -447,7 +480,7 @@
             device_id=(lax.rem(my_row + members, n_rows), my_col),
             device_id_type=MESH,
         )
-        for k in range(STAGES)
+        for k in range(stages)
     ]
 
     @pl.when(group_of == 0)
@@ -465,7 +498,7 @@
                 entered = pushed if entered is None else jnp.exp(end) * entered + pushed
             down_out[k, c] = entered.astype(bf16)
 
-    for k in range(STAGES):
+    for k in range(stages):
         for h in range(HALVES):
             across[h][k][1]()
         first_token = k * stage_tokens
@@ -484,8 +517,8 @@
         for g in range(k * stage_chunks, (k + 1) * stage_chunks):
             y_all[g * chunk : (g + 1) * chunk, :] = within(g, skips_d)
 
-    back = [exchange(send2.at[k], recv2.at[k], STAGES * HALVES + k, ()) for k in range(STAGES)]
-    for k in range(STAGES):
+    back = [exchange(send2.at[k], recv2.at[k], stages * HALVES + k, ()) for k in range(stages)]
+    for k in range(stages):
 
         @pl.when(group_of > 0)
         def _():
@@ -504,7 +537,7 @@
         send2[k] = shaped(mm_tn(to_columns, jnp.concatenate(parts, axis=0)), send2.shape[1:])
         back[k][0]()
 
-    for k in range(STAGES):
+    for k in range(stages):
         back[k][1]()
         z = flat(recv2[k]).astype(f32)
         scale = lax.rsqrt(jnp.mean(z * z, axis=-1, keepdims=True) + 1e-5)
@@ -516,7 +549,7 @@
         out_ref[h * half_rows : (h + 1) * half_rows] = mixed.reshape(half_rows, width, feats)
 
     for h in range(HALVES):
-        for k in range(STAGES):
+        for k in range(stages):
             across[h][k][2]()
 
     @pl.when(group_of < GROUPS - 1)
@@ -538,9 +571,10 @@
     states = (args[3].shape[0] - heads) // 2
     chunks = local_rows
     members = n_rows // GROUPS
-    stage_lines = width // members // STAGES
-    piece = (STAGES, members, HALVES, local_rows // HALVES * stage_lines, feats)
-    down = (STAGES, stage_lines, states, feats)
+    stages = min(MOST_STAGES, width // members)
+    stage_lines = width // members // stages
+    piece = (stages, members, HALVES, local_rows // HALVES * stage_lines, feats)
+    down = (stages, stage_lines, states, feats)
     big = (tokens, feats)
     vmem = pl.BlockSpec(memory_space=pltpu.VMEM)
     return pl.pallas_call(
@@ -569,16 +603,16 @@
             pltpu.VMEM(piece, bf16),
             pltpu.VMEM(piece, bf16),
             pltpu.VMEM(piece, bf16),
-            pltpu.SemaphoreType.DMA((STAGES * (HALVES + 1), members)),
-            pltpu.SemaphoreType.DMA((STAGES * (HALVES + 1), members)),
+            pltpu.SemaphoreType.DMA((stages * (HALVES + 1), members)),
+            pltpu.SemaphoreType.DMA((stages * (HALVES + 1), members)),
             pltpu.SemaphoreType.DMA((2, HALVES)),
             pltpu.VMEM(down, bf16),
             pltpu.VMEM(down, bf16),
-            pltpu.SemaphoreType.DMA((2, STAGES)),
-            pltpu.SemaphoreType.DMA((len(args),)),
+            pltpu.SemaphoreType.DMA((2, stages)),
+            pltpu.SemaphoreType.DMA((len(args) + HALVES,)),
         ],
         compiler_params=pltpu.CompilerParams(
-            collective_id=0, has_side_effects=True, vmem_limit_bytes=32 * 1024 * 1024
+            collective_id=0, has_side_effects=True, vmem_limit_bytes=425 * 128 * 1024
         ),
     )(*args)
 

time: 36.7 us -> 32.6 us (0.89)
  local copies, waits for them, and re-layouts: 7.24 us -> 3.08 us
    unnamed x31 -> x23, local copies, waits for them, and re-layouts: 7.24 us -> 3.08 us
where the time goes in v5:
time: 32.6 us; the launch traced here: 32.4 us
  Pallas kernels  29.2 us (90%)
  local copies, waits for them, and re-layouts  3.08 us (9%)
    pallas_call x1, Pallas kernels, on_device(): pl.pallas_call(functools.partial(block_kernel, n_rows, n_cols), out_shape...  29.2 us
    unnamed x23, local copies, waits for them, and re-layouts  3.08 us

profile of v5, /device:TPU:23, one launch (start us, length us, event | category | flops | bytes accessed | tf_op | source)
XLA Modules:
  0.0 32.4 jit_solution(3306614671928947157)
XLA Ops:
  0.0 0.0 copy-start.7
  0.0 0.0 copy-start.8
  0.0 0.0 copy-start.9
  0.0 0.0 copy-start.10
  0.0 0.0 copy-start.4
  0.0 0.0 copy-start.2
  0.0 0.0 copy-start.3
  0.0 0.0 copy-start.5
  0.1 0.0 copy-start.6
  0.1 0.6 %copy-done.7 = f32[8]{0:T(128)S(1)} copy-done((f32[8]{0:T(128)S(1)}, f32[8]{0:T(128)}, u32[]{:S(2)}) %copy-start.7) | copy-done | bytes 56
  0.7 0.0 copy-done.8
  0.7 0.0 copy-done.9
  0.7 0.0 copy-done.10
  0.7 0.0 copy-done.4
  0.7 0.0 copy-done.2
  0.8 0.0 copy-done.3
  0.8 0.0 copy-done.5
  0.8 0.0 copy-done.6
  0.8 0.0 copy-start
  0.8 0.8 %copy-done = bf16[512,40]{0,1:T(8,128)(2,1)S(1)} copy-done((bf16[512,40]{0,1:T(8,128)(2,1)S(1)}, bf16[512,40]{0,1:T(8,128)(2,1)}, u32[]{:S(2)}) %copy-start) | copy-done | bytes 40984
  1.6 0.0 copy-start.1
  1.6 0.8 %copy-done.1 = bf16[512,40]{0,1:T(8,128)(2,1)S(1)} copy-done((bf16[512,40]{0,1:T(8,128)(2,1)S(1)}, bf16[512,40]{0,1:T(8,128)(2,1)}, u32[]{:S(2)}) %copy-start.1) | copy-done | bytes 40984
  2.3 29.2 %shard_map.145 = bf16[8,64,512]{2,1,0:T(8,128)(2,1)S(1)} custom-call(bf16[8,64,512]{2,1,0:T(8,128)(2,1)} %refs_0_.1, s32[8,64]{1,0:T(8,128)S(1)} %copy-done.2, bf16[512,512]{1,0:T(8,128)(2,1)} %refs_2_.1, bf16[40,512]{1,0:T(8,128)(2,1)S(1)} %bitcast.10, bf16[40,512]{1,0:T(8,128)(2,1)S(1)} %bitcast.11, bf16[512,512]{1,0:T(8,128)(2,1)} %refs_5_.1, ...), custom_call_target="tpu_custom_call" | custom-call | tf_op jit(solution)/shard_map/pallas_call | solution.py:580
  31.6 0.8 %copy.17 = bf16[8,64,512]{2,1,0:T(8,128)(2,1)} copy(bf16[8,64,512]{2,1,0:T(8,128)(2,1)S(1)} %shard_map.145) | data formatting | bytes 1048576
Async XLA Ops:
  0.0 0.7 %copy-start.7 = (f32[8]{0:T(128)S(1)}, f32[8]{0:T(128)}, u32[]{:S(2)}) copy-start(f32[8]{0:T(128)} %param.24) | copy-start | bytes 100
  0.0 0.7 %copy-start.8 = (f32[8]{0:T(128)S(1)}, f32[8]{0:T(128)}, u32[]{:S(2)}) copy-start(f32[8]{0:T(128)} %param.25) | copy-start | bytes 100
  0.0 0.7 %copy-start.9 = (f32[8]{0:T(128)S(1)}, f32[8]{0:T(128)}, u32[]{:S(2)}) copy-start(f32[8]{0:T(128)} %param.26) | copy-start | bytes 100
  0.0 0.7 %copy-start.10 = (f32[8]{0:T(128)S(1)}, f32[8]{0:T(128)}, u32[]{:S(2)}) copy-start(f32[8]{0:T(128)} %param.27) | copy-start | bytes 100
  0.0 0.7 %copy-start.4 = (f32[512]{0:T(512)S(1)}, f32[512]{0:T(512)}, u32[]{:S(2)}) copy-start(f32[512]{0:T(512)} %param.29) | copy-start | bytes 6148
  0.0 0.7 %copy-start.2 = (s32[8,64]{1,0:T(8,128)S(1)}, s32[8,64]{1,0:T(8,128)}, u32[]{:S(2)}) copy-start(s32[8,64]{1,0:T(8,128)} %refs_1_.1) | copy-start | bytes 6148
  0.0 0.7 %copy-start.3 = (f32[512]{0:T(512)S(1)}, f32[512]{0:T(512)}, u32[]{:S(2)}) copy-start(f32[512]{0:T(512)} %param.28) | copy-start | bytes 6148
  0.0 0.7 %copy-start.5 = (f32[8]{0:T(128)S(1)}, f32[8]{0:T(128)}, u32[]{:S(2)}) copy-start(f32[8]{0:T(128)} %param.22) | copy-start | bytes 100
  0.1 0.7 %copy-start.6 = (f32[8]{0:T(128)S(1)}, f32[8]{0:T(128)}, u32[]{:S(2)}) copy-start(f32[8]{0:T(128)} %param.23) | copy-start | bytes 100
  0.8 0.8 %copy-start = (bf16[512,40]{0,1:T(8,128)(2,1)S(1)}, bf16[512,40]{0,1:T(8,128)(2,1)}, u32[]{:S(2)}) copy-start(bf16[512,40]{0,1:T(8,128)(2,1)} %param.18) | copy-start | bytes 122884
  1.6 0.8 %copy-start.1 = (bf16[512,40]{0,1:T(8,128)(2,1)S(1)}, bf16[512,40]{0,1:T(8,128)(2,1)}, u32[]{:S(2)}) copy-start(bf16[512,40]{0,1:T(8,128)(2,1)} %param.19) | copy-start | bytes 122884

commit v6 on v5

--- a/solution.py
+++ b/solution.py
@@ -279,7 +279,8 @@
         run = l_exp[rows, :]
         run_u = jnp.sum(jnp.where(diagonal, run, 0.0), axis=0, keepdims=True)
         b = b_all[rows, :]
-        cb = mm_nt(c_all[rows, :], jnp.concatenate([b] * heads, axis=0))
+        cb = mm_nt(c_all[rows, :], jnp.concatenate([b, b], axis=0))
+        cb = jnp.concatenate([cb] * (heads // 2), axis=1)
         decay = jnp.exp(jnp.where(causal, run - run_u, -1e30))
         weights = (decay * cb).astype(bf16)
         vb = v_all[rows, :]
@@ -579,7 +580,7 @@
     vmem = pl.BlockSpec(memory_space=pltpu.VMEM)
     return pl.pallas_call(
         functools.partial(block_kernel, n_rows, n_cols),
-        out_shape=jax.ShapeDtypeStruct(patches.shape, bf16),
+        out_shape=pltpu.VMEM(patches.shape, bf16),
         in_specs=[pl.BlockSpec(memory_space=pltpu.HBM)] * len(args),
         out_specs=vmem,
         scratch_shapes=[pltpu.VMEM(a.shape, a.dtype) for a in args]
@@ -612,7 +613,7 @@
             pltpu.SemaphoreType.DMA((len(args) + HALVES,)),
         ],
         compiler_params=pltpu.CompilerParams(
-            collective_id=0, has_side_effects=True, vmem_limit_bytes=425 * 128 * 1024
+            collective_id=0, has_side_effects=True, vmem_limit_bytes=56 * 1024 * 1024
         ),
     )(*args)
 

time: 32.6 us -> 30.2 us (0.926)
  local copies, waits for them, and re-layouts: 3.08 us -> 0.8 us
    unnamed x23 -> x1, local copies, waits for them, and re-layouts: 3.08 us -> 0.8 us
where the time goes in v6:
time: 30.2 us; the launch traced here: 30 us
  Pallas kernels  29.2 us (97%)
  local copies, waits for them, and re-layouts  0.8 us (3%)
    pallas_call x1, Pallas kernels, on_device(): pl.pallas_call(functools.partial(block_kernel, n_rows, n_cols), out_shape...  29.2 us
    unnamed x1, local copies, waits for them, and re-layouts  0.8 us

profile of v6, /device:TPU:23, one launch (start us, length us, event | category | flops | bytes accessed | tf_op | source)
XLA Modules:
  0.0 30.0 jit_solution(5289059339295434830)
XLA Ops:
  0.0 29.2 %shard_map.145 = bf16[8,64,512]{2,1,0:T(8,128)(2,1)S(1)} custom-call(bf16[8,64,512]{2,1,0:T(8,128)(2,1)} %refs_0_.1, s32[8,64]{1,0:T(8,128)} %refs_1_.1, bf16[512,512]{1,0:T(8,128)(2,1)} %refs_2_.1, bf16[40,512]{1,0:T(8,128)(2,1)} %bitcast.10, bf16[40,512]{1,0:T(8,128)(2,1)} %bitcast.11, bf16[512,512]{1,0:T(8,128)(2,1)} %refs_5_.1, ...), custom_call_target="tpu_custom_call" | custom-call | tf_op jit(solution)/shard_map/pallas_call | solution.py:581
  29.2 0.8 %copy.17 = bf16[8,64,512]{2,1,0:T(8,128)(2,1)} copy(bf16[8,64,512]{2,1,0:T(8,128)(2,1)S(1)} %shard_map.145) | data formatting | bytes 1048576

commit v7 on v6

--- a/solution.py
+++ b/solution.py
@@ -515,8 +515,8 @@
                 ends(k)
             hand_down[k].start()
 
-        for g in range(k * stage_chunks, (k + 1) * stage_chunks):
-            y_all[g * chunk : (g + 1) * chunk, :] = within(g, skips_d)
+    for g in range(chunks):
+        y_all[g * chunk : (g + 1) * chunk, :] = within(g, skips_d)
 
     back = [exchange(send2.at[k], recv2.at[k], stages * HALVES + k, ()) for k in range(stages)]
     for k in range(stages):

time: 30.2 us -> 30.3 us (level)
  no operation moved by 1% of the time
where the time goes in v7:
time: 30.3 us; the launch traced here: 30.1 us
  Pallas kernels  29.3 us (97%)
  local copies, waits for them, and re-layouts  0.8 us (3%)
    pallas_call x1, Pallas kernels, on_device(): pl.pallas_call(functools.partial(block_kernel, n_rows, n_cols), out_shape...  29.3 us
    unnamed x1, local copies, waits for them, and re-layouts  0.8 us

profile of v7, /device:TPU:23, one launch (start us, length us, event | category | flops | bytes accessed | tf_op | source)
XLA Modules:
  0.0 30.1 jit_solution(13906076495505014069)
XLA Ops:
  0.0 29.3 %shard_map.145 = bf16[8,64,512]{2,1,0:T(8,128)(2,1)S(1)} custom-call(bf16[8,64,512]{2,1,0:T(8,128)(2,1)} %refs_0_.1, s32[8,64]{1,0:T(8,128)} %refs_1_.1, bf16[512,512]{1,0:T(8,128)(2,1)} %refs_2_.1, bf16[40,512]{1,0:T(8,128)(2,1)} %bitcast.10, bf16[40,512]{1,0:T(8,128)(2,1)} %bitcast.11, bf16[512,512]{1,0:T(8,128)(2,1)} %refs_5_.1, ...), custom_call_target="tpu_custom_call" | custom-call | tf_op jit(solution)/shard_map/pallas_call | solution.py:581
  29.4 0.8 %copy.17 = bf16[8,64,512]{2,1,0:T(8,128)(2,1)} copy(bf16[8,64,512]{2,1,0:T(8,128)(2,1)S(1)} %shard_map.145) | data formatting | bytes 1048576

commit v8 on v7

--- a/solution.py
+++ b/solution.py
@@ -9,8 +9,8 @@
 
 MESH = pl.DeviceIdType.MESH
 GROUPS = 2
-MOST_STAGES = 2
-HALVES = 2
+MOST_STAGES = 4
+HALVES = 1
 f32 = jnp.float32
 bf16 = jnp.bfloat16
 

time: 30.3 us -> 29.4 us (0.970)
  the two profiles are of different devices: /device:TPU:23 before, /device:TPU:7 now
where the time goes in v8:
time: 29.4 us; the launch traced here: 29.2 us
  Pallas kernels  28.4 us (97%)
  local copies, waits for them, and re-layouts  0.8 us (3%)
    pallas_call x1, Pallas kernels, on_device(): pl.pallas_call(functools.partial(block_kernel, n_rows, n_cols), out_shape...  28.4 us
    unnamed x1, local copies, waits for them, and re-layouts  0.8 us

profile of v8, /device:TPU:7, one launch (start us, length us, event | category | flops | bytes accessed | tf_op | source)
XLA Modules:
  0.0 29.2 jit_solution(10197415378051024038)
XLA Ops:
  0.0 28.4 %shard_map.145 = bf16[8,64,512]{2,1,0:T(8,128)(2,1)S(1)} custom-call(bf16[8,64,512]{2,1,0:T(8,128)(2,1)} %refs_0_.1, s32[8,64]{1,0:T(8,128)} %refs_1_.1, bf16[512,512]{1,0:T(8,128)(2,1)} %refs_2_.1, bf16[40,512]{1,0:T(8,128)(2,1)} %bitcast.10, bf16[40,512]{1,0:T(8,128)(2,1)} %bitcast.11, bf16[512,512]{1,0:T(8,128)(2,1)} %refs_5_.1, ...), custom_call_target="tpu_custom_call" | custom-call | tf_op jit(solution)/shard_map/pallas_call | solution.py:581
  28.4 0.8 %copy.17 = bf16[8,64,512]{2,1,0:T(8,128)(2,1)} copy(bf16[8,64,512]{2,1,0:T(8,128)(2,1)S(1)} %shard_map.145) | data formatting | bytes 1048576
